TPU v7x, 32 devices: a whole 2x2x4 slice. The times are simulated.
32 devices in a mesh: grp: 2 (over y), gy: 4 (over z), gx: 2 (over x), col: 2 (over core).
Axes of the slice: x: 2, y: 2, z: 4, core: 2. Of those that a mesh axis runs over, the one named last changes fastest.
Arguments:
- fine_in: float32 [32, 16, 16, 256], P('col', 'grp', 'gy', 'gx'), parts along dimension 1, may hold values from -6 to 6
- context_in: float32 [64, 4, 4, 64], P('col', 'grp', 'gy', 'gx'), parts along dimension 1, may hold values from -6 to 6
- weight_fine: float32 [3, 3, 3, 32, 32], P(None, None, None, None, 'col'), may hold values from -0.21875 to 0.21875
- weight_coarse: float32 [3, 3, 3, 64, 64], P(None, None, None, None, 'col'), may hold values from -0.15625 to 0.15625
- lift_weight: float32 [64, 32], P(None, 'col'), may hold values from -0.75 to 0.75
- lower_weight: float32 [32, 64], P(None, 'col'), may hold values from -1 to 1
- block_row: int32 [8, 2], P('grp'), parts along dimension 0, may hold values from 0 to 3
- tile_count: int32 [8, 2], P('grp'), parts along dimension 0, may hold values from 1 to 4
- fine_cotangent: float32 [32, 16, 16, 256], P('col', 'grp', 'gy', 'gx'), parts along dimension 1, may hold values from -6 to 6
- coarse_cotangent: float32 [64, 4, 4, 64], P('col', 'grp', 'gy', 'gx'), parts along dimension 1, may hold values from -6 to 6
Outputs:
- joined_fine: float32 [32, 16, 16, 256], P('col', 'grp', 'gy', 'gx'), parts along dimension 1
- joined_coarse: float32 [64, 4, 4, 64], P('col', 'grp', 'gy', 'gx'), parts along dimension 1
- fine_gradient: float32 [6, 3, 3, 32, 32], P('grp', None, None, None, 'col'), parts along dimension 0
- coarse_gradient: float32 [6, 3, 3, 64, 64], P('grp', None, None, None, 'col'), parts along dimension 0
- lift_gradient: float32 [128, 32], P('grp', 'col'), parts along dimension 0
- lower_gradient: float32 [64, 64], P('grp', 'col'), parts along dimension 0
There are 2 independent parts, one for each index of `grp`. A program takes and returns all parts, laid end to end along the dimension named above; an argument that names none is the same for every part. Nothing has to cross between parts.
All inputs are finite; a program needn't handle non-finite values.
Results may differ from a plain program's by a relative error of at most 0.000093.
Values sent between devices are 32-bit elements; how exact they have to be, the bound alone decides.
A program may use at most 64 MiB of HBM per device.

v0:
```python
import functools

import jax
import jax.numpy as jnp
from jax import lax
from jax.experimental import pallas as pl
from jax.experimental.pallas import tpu as pltpu
from jax.sharding import PartitionSpec as P

RATIO = 4


precise = lax.Precision.HIGH


def pad_depth(volume):
    return jnp.pad(volume, ((0, 0), (1, 1), (0, 0), (0, 0)))


def shifted_stack(padded, shift_z, shift_y, extent_z, extent_y, extent_x):
    return jnp.stack(
        [
            padded[
                :,
                shift_z : shift_z + extent_z,
                shift_y : shift_y + extent_y,
                shift_x : shift_x + extent_x,
            ]
            for shift_x in range(3)
        ]
    )


def convolve(padded, kernel):
    extent_z = padded.shape[1] - 2
    extent_y = padded.shape[2] - 2
    extent_x = padded.shape[3] - 2
    result = jnp.zeros((kernel.shape[4], extent_z, extent_y, extent_x), jnp.float32)
    for shift_z in range(3):
        for shift_y in range(3):
            stacked = shifted_stack(padded, shift_z, shift_y, extent_z, extent_y, extent_x)
            result = result + jnp.einsum(
                "aizyx,aio->ozyx", stacked, kernel[shift_z, shift_y], precision=precise
            )
    return result


def kernel_terms(padded, seed):
    extent_z = seed.shape[1]
    extent_y = seed.shape[2]
    extent_x = seed.shape[3]
    layers_z = []
    for shift_z in range(3):
        layers_y = []
        for shift_y in range(3):
            stacked = shifted_stack(padded, shift_z, shift_y, extent_z, extent_y, extent_x)
            layers_y.append(jnp.einsum("aizyx,ozyx->aio", stacked, seed, precision=precise))
        layers_z.append(jnp.stack(layers_y))
    return jnp.stack(layers_z)


def silu_slope(value):
    logistic = jax.nn.sigmoid(value)
    return logistic * (1.0 + value * (1.0 - logistic))


def refine(block):
    channels, extent_z, extent_y, extent_x = block.shape
    grown = jnp.broadcast_to(
        block[:, :, None, :, None, :, None],
        (channels, extent_z, RATIO, extent_y, RATIO, extent_x, RATIO),
    )
    return grown.reshape(channels, extent_z * RATIO, extent_y * RATIO, extent_x * RATIO)


def group_view(volume):
    channels, extent_z, extent_y, extent_x = volume.shape
    return volume.reshape(
        channels, extent_z // RATIO, RATIO, extent_y // RATIO, RATIO, extent_x // RATIO, RATIO
    )


LANES = 128
AXES = ("gy", "gx", "col")
MESH = pl.DeviceIdType.MESH
IN_VMEM = pl.BlockSpec(memory_space=pltpu.VMEM)


def near_keys(rows, columns):
    return sorted({(a % rows, b % columns) for a in (-1, 0, 1) for b in (-1, 0, 1)})


def peer(sizes, offset):
    return {
        axis: lax.rem(lax.axis_index(axis) + step, size) if step else lax.axis_index(axis)
        for axis, size, step in zip(AXES, sizes, offset)
    }


def greet(sizes, offsets):
    barrier = pltpu.get_barrier_semaphore()
    for offset in offsets:
        pl.semaphore_signal(barrier, inc=1, device_id=peer(sizes, offset), device_id_type=MESH)
    pl.semaphore_wait(barrier, len(offsets))


def opening_plan(sizes):
    rows, columns, cores = sizes
    plan = []
    for core in range(1, cores):
        plan.append(("whole", (0, 0, core)))
    for core in range(cores):
        plan.append(("last", (1, 0, core)))
        plan.append(("first", (rows - 1, 0, core)))
    for a, b in near_keys(rows, columns):
        for core in range(cores):
            if (a, b, core) != (0, 0, 0):
                plan.append(("near", (a, b, core)))
    for a in range(rows):
        for core in range(cores):
            if (a, core) != (0, 0):
                plan.append(("line", (a, 0, core)))
    return plan


def both_ways(sizes, plan):
    found = {offset for _, offset in plan}
    found |= {tuple((n - s) % n for n, s in zip(sizes, offset)) for offset in found}
    return sorted(found)


def opening_kernel(sizes, fine, near, line, whole_out, face_out, near_out, line_out, send, recv):
    rows, columns, _ = sizes
    plan = opening_plan(sizes)
    keys = near_keys(rows, columns)
    row_here, core_here = lax.axis_index("gy"), lax.axis_index("col")
    greet(sizes, both_ways(sizes, plan))
    height = fine.shape[1]
    copies = []
    for index, (kind, offset) in enumerate(plan):
        if kind == "whole":
            ends = (fine, whole_out.at[core_here])
        elif kind == "last":
            ends = (fine.at[:, height - 1], face_out.at[0, core_here])
        elif kind == "first":
            ends = (fine.at[:, 0], face_out.at[1, core_here])
        elif kind == "near":
            slot = keys.index(((rows - offset[0]) % rows, (columns - offset[1]) % columns))
            ends = (near, near_out.at[slot, core_here])
        else:
            ends = (line, line_out.at[row_here, core_here])
        copy = pltpu.make_async_remote_copy(
            src_ref=ends[0],
            dst_ref=ends[1],
            send_sem=send.at[index],
            recv_sem=recv.at[index],
            device_id=peer(sizes, offset),
            device_id_type=MESH,
        )
        copy.start()
        copies.append(copy)
    whole_out[core_here] = fine[...]
    near_out[keys.index((0, 0)), core_here] = near[...]
    line_out[row_here, core_here] = line[...]
    for copy in copies:
        copy.wait()


def opening(sizes, fine, near, line):
    rows, columns, cores = sizes
    number = len(opening_plan(sizes))
    depth, _, channels, wide = fine.shape
    return pl.pallas_call(
        functools.partial(opening_kernel, sizes),
        out_shape=(
            jax.ShapeDtypeStruct((cores, *fine.shape), jnp.float32),
            jax.ShapeDtypeStruct((2, cores, depth, channels, wide), jnp.float32),
            jax.ShapeDtypeStruct((len(near_keys(rows, columns)), cores, *near.shape), jnp.float32),
            jax.ShapeDtypeStruct((rows, cores, *line.shape), jnp.float32),
        ),
        in_specs=[IN_VMEM] * 3,
        out_specs=[IN_VMEM] * 4,
        scratch_shapes=[pltpu.SemaphoreType.DMA((number,)), pltpu.SemaphoreType.DMA((number,))],
        compiler_params=pltpu.CompilerParams(
            collective_id=0, has_side_effects=True, vmem_limit_bytes=48 << 20
        ),
    )(fine, near, line)


def line_kernel(sizes, line, line_out, send, recv):
    rows, _, cores = sizes
    offsets = [(a, 0, c) for a in range(rows) for c in range(cores) if (a, c) != (0, 0)]
    row_here, core_here = lax.axis_index("gy"), lax.axis_index("col")
    greet(sizes, offsets)
    copies = []
    for index, offset in enumerate(offsets):
        copy = pltpu.make_async_remote_copy(
            src_ref=line,
            dst_ref=line_out.at[row_here, core_here],
            send_sem=send.at[index],
            recv_sem=recv.at[index],
            device_id=peer(sizes, offset),
            device_id_type=MESH,
        )
        copy.start()
        copies.append(copy)
    line_out[row_here, core_here] = line[...]
    for copy in copies:
        copy.wait()


def line_gather(sizes, line):
    rows, _, cores = sizes
    number = rows * cores - 1
    return pl.pallas_call(
        functools.partial(line_kernel, sizes),
        out_shape=jax.ShapeDtypeStruct((rows, cores, *line.shape), jnp.float32),
        in_specs=[IN_VMEM],
        out_specs=IN_VMEM,
        scratch_shapes=[pltpu.SemaphoreType.DMA((number,)), pltpu.SemaphoreType.DMA((number,))],
        compiler_params=pltpu.CompilerParams(collective_id=1, has_side_effects=True),
    )(line)


def total_kernel(sizes, parts, result, landed, send, recv, send_back, recv_back):
    rows, columns, _ = sizes
    offsets = [(a, b, 0) for a in range(rows) for b in range(columns) if (a, b) != (0, 0)]

    def place(offset):
        target = peer(sizes, offset)
        return target["gy"] * columns + target["gx"]

    here = lax.axis_index("gy") * columns + lax.axis_index("gx")
    greet(sizes, offsets)
    copies = []
    for index, offset in enumerate(offsets):
        copy = pltpu.make_async_remote_copy(
            src_ref=parts.at[place(offset)],
            dst_ref=landed.at[index],
            send_sem=send.at[index],
            recv_sem=recv.at[index],
            device_id=peer(sizes, offset),
            device_id_type=MESH,
        )
        copy.start()
        copies.append(copy)
    total = parts[here]
    for index, copy in enumerate(copies):
        copy.wait()
        total = total + landed[index]
    result[here] = total
    copies = []
    for index, offset in enumerate(offsets):
        copy = pltpu.make_async_remote_copy(
            src_ref=result.at[here],
            dst_ref=result.at[here],
            send_sem=send_back.at[index],
            recv_sem=recv_back.at[index],
            device_id=peer(sizes, offset),
            device_id_type=MESH,
        )
        copy.start()
        copies.append(copy)
    for copy in copies:
        copy.wait()


def total_over_tiles(sizes, arrays):
    rows, columns, _ = sizes
    peers = rows * columns
    flat = jnp.concatenate([array.reshape(-1, LANES) for array in arrays])
    chunk = -(-flat.shape[0] // (8 * peers)) * 8
    parts = jnp.pad(flat, ((0, peers * chunk - flat.shape[0]), (0, 0))).reshape(peers, chunk, LANES)
    number = peers - 1
    result = pl.pallas_call(
        functools.partial(total_kernel, sizes),
        out_shape=jax.ShapeDtypeStruct(parts.shape, jnp.float32),
        in_specs=[IN_VMEM],
        out_specs=IN_VMEM,
        scratch_shapes=[pltpu.VMEM((number, chunk, LANES), jnp.float32)]
        + [pltpu.SemaphoreType.DMA((number,))] * 4,
        compiler_params=pltpu.CompilerParams(collective_id=2, has_side_effects=True),
    )(parts)
    result = result.reshape(peers * chunk, LANES)
    given, start = [], 0
    for array in arrays:
        count = array.size // LANES
        given.append(result[start : start + count].reshape(array.shape))
        start += count
    return tuple(given)


def as_rows(*arrays):
    return jnp.concatenate([array.reshape(-1, LANES) for array in arrays])


def local(
    sizes,
    fine_in,
    context_in,
    weight_fine,
    weight_coarse,
    lift_weight,
    lower_weight,
    block_row,
    tile_count,
    fine_cotangent,
    coarse_cotangent,
):
    rows_total, columns_total, cores = sizes
    column_here, row_here, core_here = (lax.axis_index(a) for a in ("gx", "gy", "col"))
    column_rows = lax.dynamic_slice_in_dim(block_row, column_here, 1, 1)[:, 0]
    column_counts = lax.dynamic_slice_in_dim(tile_count, column_here, 1, 1)[:, 0].astype(
        jnp.float32
    )
    target = lax.dynamic_slice_in_dim(column_rows, row_here, 1, 0)[0]
    own_count = lax.dynamic_slice_in_dim(column_counts, row_here, 1, 0)[0]
    routed_here = (column_rows == row_here).astype(jnp.float32)
    weights_here = routed_here * column_counts
    divisor_here = jnp.maximum(jnp.sum(weights_here), 1.0)
    divisor_target = jnp.maximum(
        jnp.sum(jnp.where(column_rows == target, column_counts, 0.0)), 1.0
    )
    channels, depth, height, wide = fine_in.shape
    broad, low, short, narrow = context_in.shape
    fine_cells = depth * height * rows_total * wide * columns_total
    coarse_cells = low * short * rows_total * narrow * columns_total
    fine_seed = fine_cotangent * fine_cells ** (-0.5)
    coarse_seed_own = coarse_cotangent * coarse_cells ** (-0.5)
    group_seed = jnp.sum(group_view(fine_seed), axis=(2, 4, 6))

    fine_rows = fine_in.transpose(1, 2, 0, 3)
    edges = jnp.stack([fine_in[..., 0], fine_in[..., wide - 1]])
    near = as_rows(context_in, edges)
    line = as_rows(coarse_seed_own, group_seed, lift_weight, lower_weight)
    whole, faces, nears, lines = opening(sizes, fine_rows, near, line)

    keys = near_keys(rows_total, columns_total)
    context_rows = context_in.size // LANES
    contexts = nears[:, :, :context_rows].reshape(
        len(keys), cores * broad, low, short, narrow
    )
    sides = nears[:, :, context_rows:].reshape(len(keys), cores, 2, channels, depth, height)

    def inside(a, b):
        row, column = row_here + a, column_here + b
        return (row >= 0) & (row < rows_total) & (column >= 0) & (column < columns_total)

    def key(a, b):
        return keys.index((a % rows_total, b % columns_total))

    def kept(a, b, value):
        return value if a == 0 and b == 0 else jnp.where(inside(a, b), value, 0.0)

    def context_piece(a, b):
        block = contexts[key(a, b)]
        block = block[:, :, -1:] if a < 0 else block[:, :, :1] if a > 0 else block
        block = block[..., -1:] if b < 0 else block[..., :1] if b > 0 else block
        return kept(a, b, block)

    coarse_pad = pad_depth(
        jnp.concatenate(
            [
                jnp.concatenate([context_piece(a, b) for b in (-1, 0, 1)], axis=3)
                for a in (-1, 0, 1)
            ],
            axis=2,
        )
    )

    def edge_piece(a, b):
        edge = sides[key(a, b), :, 1 if b < 0 else 0].reshape(cores * channels, depth, height)
        edge = edge[:, :, -1:] if a < 0 else edge[:, :, :1] if a > 0 else edge
        return kept(a, b, edge)[..., None]

    def edge_column(b):
        return jnp.concatenate([edge_piece(a, b) for a in (-1, 0, 1)], axis=2)

    def face(a):
        rows = faces[0 if a < 0 else 1].transpose(0, 2, 1, 3).reshape(cores * channels, depth, wide)
        return kept(a, 0, rows)[:, :, None]

    fine_all = whole.transpose(0, 3, 1, 2, 4).reshape(cores * channels, depth, height, wide)
    fine_pad = pad_depth(
        jnp.concatenate(
            [
                edge_column(-1),
                jnp.concatenate([face(-1), fine_all, face(1)], axis=2),
                edge_column(1),
            ],
            axis=3,
        )
    )

    first = coarse_cotangent.size // LANES
    second = first + group_seed.size // LANES
    third = second + lift_weight.size // LANES
    seeds = lines[:, :, :first].reshape(rows_total, cores * broad, low, short, narrow)
    groups = lines[:, :, first:second].reshape(
        rows_total, cores * channels, low, short, narrow
    )
    weights_all = lax.dynamic_index_in_dim(lines, row_here, 0, False)
    lift_all = weights_all[:, second:third].reshape(cores, *lift_weight.shape)
    lower_all = weights_all[:, third:].reshape(cores, *lower_weight.shape)

    lifted_seed_all = jnp.einsum("r,rfzyx->fzyx", routed_here, groups, precision=lax.Precision.HIGHEST)
    lifted_seed = lax.dynamic_slice_in_dim(lifted_seed_all, core_here * channels, channels, 0)
    lift_own = lax.dynamic_slice_in_dim(lift_all, core_here * broad, broad, 1)
    coarse_total_seed = coarse_seed_own + jnp.einsum(
        "kcf,kfzyx->czyx",
        lift_own,
        lifted_seed_all.reshape(cores, channels, low, short, narrow),
        precision=precise,
    )
    lower_own = lax.dynamic_slice_in_dim(lower_all, core_here * channels, channels, 1)
    target_seed = lax.dynamic_index_in_dim(seeds, target, 0, False)
    tile_seed = jnp.einsum(
        "kfc,kczyx->fzyx",
        lower_own,
        target_seed.reshape(cores, broad, low, short, narrow),
        precision=precise,
    ) * (own_count / (RATIO * RATIO * RATIO) / divisor_target)

    coarse_pre = convolve(coarse_pad, weight_coarse)
    coarse_hidden = jax.nn.silu(coarse_pre)
    fine_pre = convolve(fine_pad, weight_fine)
    fine_hidden = jax.nn.silu(fine_pre)
    tile_means = group_view(fine_hidden).mean(axis=(2, 4, 6))
    middle = line_gather(sizes, as_rows(coarse_hidden, tile_means))
    hiddens = middle[:, :, :first].reshape(rows_total, cores * broad, low, short, narrow)
    means = middle[:, :, first:].reshape(rows_total, cores * channels, low, short, narrow)
    coarse_wide = lax.dynamic_index_in_dim(hiddens, row_here, 0, False)
    chosen = jnp.einsum(
        "czyx,cf->fzyx",
        lax.dynamic_index_in_dim(hiddens, target, 0, False),
        lift_weight,
        precision=precise,
    )
    joined_fine = fine_hidden + refine(chosen)
    averaged_wide = (
        jnp.einsum("r,rfzyx->fzyx", weights_here, means, precision=lax.Precision.HIGHEST) / divisor_here
    )
    joined_coarse = coarse_hidden + jnp.einsum(
        "fzyx,fc->czyx", averaged_wide, lower_weight, precision=precise
    )
    lower_gradient = jnp.einsum("fzyx,czyx->fc", averaged_wide, coarse_seed_own, precision=precise)
    lift_gradient = jnp.einsum("czyx,fzyx->cf", coarse_wide, lifted_seed, precision=precise)
    hidden_seed = fine_seed + refine(tile_seed)
    coarse_gradient = kernel_terms(coarse_pad, coarse_total_seed * silu_slope(coarse_pre))
    fine_gradient = kernel_terms(fine_pad, hidden_seed * silu_slope(fine_pre))
    fine_gradient, coarse_gradient, lift_gradient, lower_gradient = total_over_tiles(
        sizes, (fine_gradient, coarse_gradient, lift_gradient, lower_gradient)
    )
    return (
        joined_fine,
        joined_coarse,
        fine_gradient,
        coarse_gradient,
        lift_gradient,
        lower_gradient,
    )


def solution(mesh):
    sizes = tuple(mesh.shape[axis] for axis in AXES)
    in_specs = (
        P("col", "grp", "gy", "gx"),
        P("col", "grp", "gy", "gx"),
        P(None, None, None, None, "col"),
        P(None, None, None, None, "col"),
        P(None, "col"),
        P(None, "col"),
        P("grp", None),
        P("grp", None),
        P("col", "grp", "gy", "gx"),
        P("col", "grp", "gy", "gx"),
    )
    out_specs = (
        P("col", "grp", "gy", "gx"),
        P("col", "grp", "gy", "gx"),
        P("grp", None, None, None, "col"),
        P("grp", None, None, None, "col"),
        P("grp", "col"),
        P("grp", "col"),
    )
    return jax.shard_map(
        functools.partial(local, sizes),
        mesh=mesh,
        in_specs=in_specs,
        out_specs=out_specs,
        check_vma=False,
    )
```

profile of v0, /device:TPU:0, one launch (start us, length us, event | category | flops | bytes accessed | tf_op | source)
XLA Modules:
  0.0 134.7 jit_solution(14730578819914117741)
XLA Ops:
  0.7 1.2 copy.996
  1.8 1.3 fusion.153
  7.2 18.3 %shard_map.145 = (f32[2,8,4,16,128]{4,3,2,1,0:T(8,128)S(1)}, f32[2,2,8,16,128]{4,3,2,1,0:T(8,128)S(1)}, f32[6,2,24,128]{3,2,1,0:T(8,128)S(1)}, f32[4,2,40,128]{3,2,1,0:T(8,128)S(1)}) custom-call(f32[8,4,16,128]{3,2,1,0:T(8,128)S(1)} %bitcast.671, f32[24,128]{1,0:T(8,128)S(1)} %pad_maximum_fusion.22.near, f32[40,128]{1,0:T(8,128)S(1)} %pad_maximum_fusion.21.line), custom_call_target="tpu_custom_call" | custom-call | tf_op jit(solution)/shard_map/pallas_call | solution.py:173
  25.5 1.6 %reshape.380 = f32[6,2,2,16,8,4]{5,4,3,2,1,0:T(8,128)S(1)} reshape(f32[6,2,8,128]{3,2,1,0:T(8,128)S(1)} %slice.435) | data formatting | bytes 98304 | tf_op jit(solution)/shard_map/reshape | solution.py:343
  27.1 0.8 fusion.150
  29.4 1.1 fusion.151
  31.2 1.9 %copy.768 = f32[32,8,4,1]{3,0,2,1:T(8,128)S(1)} copy(f32[32,8,4,1]{2,1,0,3:T(8,128)S(1)} %bitcast.686) | data formatting | bytes 8192 | tf_op jit(solution)/shard_map/jit(_where)/select_n | solution.py:353
  33.8 1.9 %copy.756 = f32[32,8,4,1]{3,0,2,1:T(8,128)S(1)} copy(f32[32,8,4,1]{2,1,0,3:T(8,128)S(1)} %bitcast.685) | data formatting | bytes 8192 | tf_op jit(solution)/shard_map/jit(_where)/select_n | solution.py:353
  37.5 4.9 %slice_bitcast_fusion.23 = (f32[1,32,8,4,128]{4,1,0,3,2:T(8,128)}, f32[1,32,8,4,128]{4,1,3,2,0:T(8,128)}, f32[1,32,8,4,128]{4,1,3,2,0:T(8,128)}, f32[1,32,8,4,12...) fusion(f32[32,10,6,130]{3,0,2,1:T(8,128)S(1)} %fusion), kind=kLoop, calls=%fused_computation.122 | loop fusion | bytes 18874368 | tf_op jit(solution)/shard_map/stack | solution.py:21
  42.4 2.3 %fusion.2 = f32[8,4,128,16,1]{2,3,0,1,4:T(8,128)S(1)} fusion(f32[3,3,3,32,16]{3,4,2,1,0:T(8,128)} %param.12, f32[1,32,8,4,128]{4,1,3,2,0:T(8,128)} %get-tuple-element.83, f32[1,32,8,4,128]{4,1,3,2,0:T(8,128)} %get-tuple-element.67, f32[1,32,8,4,128]{4,1,3,2,0:T(8,128)} %get-tuple-element.68), kind=kOutput, calls=%fused_computation.20 | convolution fusion | flops 38535168 | bytes 1859584 | tf_op jit(solution)/shard_map/aizyx,aio->ozyx/dot_general | solution.py:42
  44.7 1.6 %pad_maximum_fusion.7 = (f32[3,32,8,4,128]{4,1,3,2,0:T(8,128)S(1)}, f32[3,32,8,4,128]{4,1,3,2,0:T(8,128)S(1)}) fusion(f32[1,32,8,4,128]{4,1,3,2,0:T(8,128)S(1)} %copy-done.8, f32[1,32,8,4,128]{4,1,3,2,0:T(8,128)S(1)} %copy-done.10, f32[1,32,8,4,128]{4,1,3,2,0:T(8,128)S(1)} %copy-done.12, f32[1,32,8,4,128]{4,1,3,2,0:T(8,128)S(1)} %copy-done.14, ...), kind=kLoop, calls=%fused_computation.17 | loop fusion | flops 1572864 | bytes 6291456 | tf_op jit(solution)/shard_map/stack | solution.py:21
  54.9 1.3 fusion.76
  59.2 1.8 %fusion.126 = (f32[]{:T(128)}, f32[]{:T(128)}, s32[4,1]{0,1:T(1,128)}, f32[4,1]{0,1:T(1,128)S(1)}) fusion(s32[]{:T(128)} %bitcast.162, s32[]{:T(128)S(6)} %axis_index.33, s32[4,2]{0,1:T(2,128)S(1)} %copy-done.71, s32[]{:T(128)S(6)} %select_n.274, s32[4,2]{0,1:T(2,128)S(1)} %copy-done.72), kind=kLoop, calls=%fused_computation.295 | loop fusion | flops 26 | bytes 84 | tf_op jit(solution)/shard_map/reduce_sum | solution.py:322
  70.6 1.6 %fusion.97 = (f32[32,2,32]{0,2,1:T(8,128)S(1)}, f32[32,2,32]{0,2,1:T(8,128)}) fusion(f32[2,32,32]{2,1,0:T(8,128)S(1)} %convolution_bitcast_fusion.13, f32[2,32,32]{2,1,0:T(8,128)S(1)} %convolution_bitcast_fusion.14, f32[2,32,32]{2,1,0:T(8,128)} %convolution_bitcast_fusion.15, f32[2,32,32]{2,1,0:T(8,128)} %convolution_bitcast_fusion.16, ...), kind=kOutput, calls=%fused_computation.238 | convolution fusion | flops 2408448 | bytes 352256 | tf_op jit(solution)/shard_map/aizyx,aio->ozyx/dot_general | solution.py:42
  72.4 1.3 pad_maximum_fusion.23.line
  73.7 7.7 %shard_map.146 = f32[4,2,24,128]{3,2,1,0:T(8,128)} custom-call(f32[24,128]{1,0:T(8,128)} %pad_maximum_fusion.23.line), custom_call_target="tpu_custom_call" | custom-call | tf_op jit(solution)/shard_map/pallas_call | solution.py:215
  81.4 0.9 slice.528
  84.4 1.9 %multiply_bitcast_fusion = (f32[16,8,4,128,1]{3,0,2,1,4:T(8,128)}, f32[16,8,4,128]{3,0,2,1:T(8,128)S(1)}) fusion(f32[16,8,4,128]{3,0,2,1:T(8,128)} %get-tuple-element.157, f32[16,8,4,128]{3,2,1,0:T(4,128)S(1)} %copy-done.24, f32[16,8,128]{2,0,1:T(8,128)S(1)} %copy.808, f32[16,8,128]{2,0,1:T(8,128)} %copy.804), kind=kLoop, calls=%fused_computation.133 | loop fusion | flops 786432 | bytes 1179648 | tf_op jit(solution)/shard_map/mul | solution.py:450
  93.5 2.9 %convolution_bitcast_fusion.22 = f32[1,3,32,16]{2,3,1,0:T(8,128)S(1)} fusion(f32[16,8,4,128,1]{3,0,2,1,4:T(8,128)} %get-tuple-element.104, f32[1,32,8,4,128]{4,1,3,2,0:T(8,128)} %get-tuple-element.83, f32[1,32,8,4,128]{4,1,3,2,0:T(8,128)} %get-tuple-element.67, f32[1,32,8,4,128]{4,1,3,2,0:T(8,128)} %get-tuple-element.68), kind=kOutput, calls=%fused_computation.83 | convolution fusion | flops 38535168 | bytes 1841152 | tf_op jit(solution)/shard_map/aizyx,ozyx->aio/dot_general | solution.py:57
  96.5 1.3 convolution_bitcast_fusion.23
  97.9 1.3 convolution_bitcast_fusion.24
  99.3 1.5 %convolution_bitcast_fusion.25 = f32[1,3,32,16]{2,3,1,0:T(8,128)S(1)} fusion(f32[16,8,4,128,1]{3,0,2,1,4:T(8,128)S(1)} %copy-done.58, f32[1,32,8,4,128]{4,1,3,2,0:T(8,128)S(1)} %copy-done.42, f32[1,32,8,4,128]{4,1,3,2,0:T(8,128)S(1)} %copy-done.48, f32[1,32,8,4,128]{4,1,3,2,0:T(8,128)S(1)} %copy-done.44), kind=kOutput, calls=%fused_computation.86 | convolution fusion | flops 38535168 | bytes 1841152 | tf_op jit(solution)/shard_map/aizyx,ozyx->aio/dot_general | solution.py:57
  100.9 1.3 convolution_bitcast_fusion.26
  102.3 1.3 convolution_bitcast_fusion.27
  103.7 1.3 convolution_bitcast_fusion.28
  105.1 1.3 convolution_bitcast_fusion.29
  106.4 1.3 fusion.42
  108.9 19.4 %shard_map.147 = f32[8,72,128]{2,1,0:T(8,128)} custom-call(f32[8,72,128]{2,1,0:T(8,128)} %bitcast.679), custom_call_target="tpu_custom_call" | custom-call | tf_op jit(solution)/shard_map/pallas_call | solution.py:275
  128.4 0.8 slice.598
  129.4 0.9 copy.837
  130.2 1.0 slice.599
  131.4 1.1 copy.838
  (317 shorter events, 38.3 us)
Async XLA Ops:
  0.6 3.9 %copy-start.63 = (f32[32,2,1,32]{3,2,1,0:T(1,128)S(1)}, f32[32,2,1,32]{3,2,1,0:T(1,128)}, u32[]{:S(2)}) copy-start(f32[32,2,1,32]{3,2,1,0:T(1,128)} %param.11) | copy-start | bytes 24580
  0.6 4.7 %copy-start.66 = (f32[32,32]{1,0:T(8,128)S(1)}, f32[32,32]{1,0:T(8,128)}, u32[]{:S(2)}) copy-start(f32[32,32]{1,0:T(8,128)} %param.15) | copy-start | bytes 12292
  0.7 4.8 %copy-start.62 = (f32[64,16]{0,1:T(8,128)S(1)}, f32[64,16]{0,1:T(8,128)}, u32[]{:S(2)}) copy-start(f32[64,16]{0,1:T(8,128)} %param.14) | copy-start | bytes 12292
  0.7 4.9 %copy-start.23 = (f32[16,8,4,128]{3,2,1,0:T(4,128)S(1)}, f32[16,8,4,128]{3,2,1,0:T(4,128)}, u32[]{:S(2)}) copy-start(f32[16,8,4,128]{3,2,1,0:T(4,128)} %param.18) | copy-start | bytes 786436
  3.1 3.2 %copy-start.64 = (f32[32,2,1,32]{3,2,1,0:T(1,128)S(1)}, f32[32,2,1,32]{3,2,1,0:T(1,128)}, u32[]{:S(2)}) copy-start(f32[32,2,1,32]{3,2,1,0:T(1,128)} %param.19) | copy-start | bytes 24580
  28.7 4.4 %copy-start.55 = (f32[1,2,1,16,8,4]{5,4,3,2,1,0:T(8,128)S(1)}, f32[1,2,1,16,8,4]{5,4,3,2,1,0:T(8,128)}, u32[]{:S(2)}) copy-start(f32[1,2,1,16,8,4]{5,4,3,2,1,0:T(8,128)} %get-tuple-element.93) | copy-start | bytes 12292
  29.4 4.1 %copy-start.54 = (f32[1,2,1,16,8,4]{5,4,3,2,1,0:T(8,128)S(1)}, f32[1,2,1,16,8,4]{5,4,3,2,1,0:T(8,128)}, u32[]{:S(2)}) copy-start(f32[1,2,1,16,8,4]{5,4,3,2,1,0:T(8,128)} %get-tuple-element.94) | copy-start | bytes 12292
  29.4 4.4 %copy-start.51 = (f32[1,2,1,16,8,4]{5,4,3,2,1,0:T(8,128)S(1)}, f32[1,2,1,16,8,4]{5,4,3,2,1,0:T(8,128)}, u32[]{:S(2)}) copy-start(f32[1,2,1,16,8,4]{5,4,3,2,1,0:T(8,128)} %get-tuple-element.95) | copy-start | bytes 12292
  30.5 5.2 %copy-start.53 = (f32[1,2,1,16,8,4]{5,4,3,2,1,0:T(8,128)S(1)}, f32[1,2,1,16,8,4]{5,4,3,2,1,0:T(8,128)}, u32[]{:S(2)}) copy-start(f32[1,2,1,16,8,4]{5,4,3,2,1,0:T(8,128)} %get-tuple-element.90) | copy-start | bytes 12292
  42.3 10.1 %copy-start = (f32[1,32,8,4,128]{4,1,3,2,0:T(8,128)}, f32[1,32,8,4,128]{4,1,3,2,0:T(8,128)S(1)}, u32[]{:S(2)}) copy-start(f32[1,32,8,4,128]{4,1,3,2,0:T(8,128)S(1)} %get-tuple-element.79) | copy-start | bytes 1572868
  42.3 10.1 %copy-start.2 = (f32[1,32,8,4,128]{4,1,3,2,0:T(8,128)}, f32[1,32,8,4,128]{4,1,3,2,0:T(8,128)S(1)}, u32[]{:S(2)}) copy-start(f32[1,32,8,4,128]{4,1,3,2,0:T(8,128)S(1)} %get-tuple-element.80) | copy-start | bytes 1572868
  48.6 3.3 %copy-start.33 = (f32[1,32,8,4,128]{4,1,3,2,0:T(8,128)}, f32[1,32,8,4,128]{4,1,3,2,0:T(8,128)S(1)}, u32[]{:S(2)}) copy-start(f32[1,32,8,4,128]{4,1,3,2,0:T(8,128)S(1)} %get-tuple-element.87) | copy-start | bytes 1572868
  48.6 3.3 %copy-start.35 = (f32[1,32,8,4,128]{4,1,3,2,0:T(8,128)}, f32[1,32,8,4,128]{4,1,3,2,0:T(8,128)S(1)}, u32[]{:S(2)}) copy-start(f32[1,32,8,4,128]{4,1,3,2,0:T(8,128)S(1)} %get-tuple-element.166) | copy-start | bytes 1572868
  54.9 4.3 %copy-start.72 = (s32[4,2]{0,1:T(2,128)S(1)}, s32[4,2]{0,1:T(2,128)}, u32[]{:S(2)}) copy-start(s32[4,2]{0,1:T(2,128)} %param.17) | copy-start | bytes 100
  70.3 14.2 %copy-start.24 = (f32[16,8,4,128]{3,2,1,0:T(4,128)S(1)}, f32[16,8,4,128]{3,2,1,0:T(4,128)}, u32[]{:S(2)}) copy-start(f32[16,8,4,128]{3,2,1,0:T(4,128)} %param.18) | copy-start | bytes 786436
  83.2 4.0 %slice-start = ((f32[4,2,24,128]{3,2,1,0:T(8,128)}), f32[4,2,8,128]{3,2,1,0:T(8,128)S(1)}, s32[]{:S(2)}) async-start(f32[4,2,24,128]{3,2,1,0:T(8,128)} %shard_map.146), calls=%async_computation | async-start | bytes 65536 | tf_op jit(solution)/shard_map/slice | solution.py:431
  83.4 3.9 %copy-start.68 = (s32[4,1]{0,1:T(1,128)S(1)}, s32[4,1]{0,1:T(1,128)}, u32[]{:S(2)}) copy-start(s32[4,1]{0,1:T(1,128)} %get-tuple-element.64) | copy-start | bytes 52
  83.4 3.9 %copy-start.70 = (f32[4,1]{0,1:T(1,128)S(1)}, f32[4,1]{0,1:T(1,128)}, u32[]{:S(2)}) copy-start(f32[4,1]{0,1:T(1,128)} %copy-done.69) | copy-start | bytes 52
  83.6 5.7 %copy-start.60 = (f32[32,2,1,32]{0,3,1,2:T(8,128)S(1)}, f32[32,2,1,32]{0,3,1,2:T(8,128)}, u32[]{:S(2)}) copy-start(f32[32,2,1,32]{0,3,1,2:T(8,128)} %copy-done.59) | copy-start | bytes 24580
  84.4 3.9 %copy-start.65 = (f32[32,2,32]{0,2,1:T(8,128)S(1)}, f32[32,2,32]{0,2,1:T(8,128)}, u32[]{:S(2)}) copy-start(f32[32,2,32]{0,2,1:T(8,128)} %get-tuple-element.159) | copy-start | bytes 24580
  84.4 3.9 %copy-start.67 = (f32[32,32]{1,0:T(8,128)S(1)}, f32[32,32]{1,0:T(8,128)}, u32[]{:S(2)}) copy-start(f32[32,32]{1,0:T(8,128)} %param.15) | copy-start | bytes 12292
  84.4 5.1 %copy-start.57 = (f32[1,64,2,1,32]{4,2,1,0,3:T(2,128)S(1)}, f32[1,64,2,1,32]{4,2,1,0,3:T(2,128)}, u32[]{:S(2)}) copy-start(f32[1,64,2,1,32]{4,2,1,0,3:T(2,128)} %get-tuple-element.106) | copy-start | bytes 49156
  93.2 3.2 %copy-start.16 = (f32[1,32,8,4,128]{4,1,3,2,0:T(8,128)S(1)}, f32[1,32,8,4,128]{4,1,3,2,0:T(8,128)}, u32[]{:S(2)}) copy-start(f32[1,32,8,4,128]{4,1,3,2,0:T(8,128)} %get-tuple-element.70) | copy-start | bytes 1572868
  93.5 3.0 %copy-start.15 = (f32[1,32,8,4,128]{4,1,3,2,0:T(8,128)S(1)}, f32[1,32,8,4,128]{4,1,3,2,0:T(8,128)}, u32[]{:S(2)}) copy-start(f32[1,32,8,4,128]{4,1,3,2,0:T(8,128)} %get-tuple-element.69) | copy-start | bytes 1572868
  93.5 3.0 %copy-start.17 = (f32[1,32,8,4,128]{4,1,3,2,0:T(8,128)S(1)}, f32[1,32,8,4,128]{4,1,3,2,0:T(8,128)}, u32[]{:S(2)}) copy-start(f32[1,32,8,4,128]{4,1,3,2,0:T(8,128)} %get-tuple-element.71) | copy-start | bytes 1572868
  93.5 3.0 %copy-start.58 = (f32[16,8,4,128,1]{3,0,2,1,4:T(8,128)S(1)}, f32[16,8,4,128,1]{3,0,2,1,4:T(8,128)}, u32[]{:S(2)}) copy-start(f32[16,8,4,128,1]{3,0,2,1,4:T(8,128)} %get-tuple-element.104) | copy-start | bytes 786436
  93.5 4.3 %copy-start.9 = (f32[1,32,8,4,128]{4,1,3,2,0:T(8,128)S(1)}, f32[1,32,8,4,128]{4,1,3,2,0:T(8,128)}, u32[]{:S(2)}) copy-start(f32[1,32,8,4,128]{4,1,3,2,0:T(8,128)} %get-tuple-element.72) | copy-start | bytes 1572868
  93.5 4.3 %copy-start.11 = (f32[1,32,8,4,128]{4,1,3,2,0:T(8,128)S(1)}, f32[1,32,8,4,128]{4,1,3,2,0:T(8,128)}, u32[]{:S(2)}) copy-start(f32[1,32,8,4,128]{4,1,3,2,0:T(8,128)} %get-tuple-element.73) | copy-start | bytes 1572868
  93.5 4.3 %copy-start.13 = (f32[1,32,8,4,128]{4,1,3,2,0:T(8,128)S(1)}, f32[1,32,8,4,128]{4,1,3,2,0:T(8,128)}, u32[]{:S(2)}) copy-start(f32[1,32,8,4,128]{4,1,3,2,0:T(8,128)} %get-tuple-element.74) | copy-start | bytes 1572868
  99.3 3.0 %copy-start.34 = (f32[1,32,8,4,128]{4,1,3,2,0:T(8,128)S(1)}, f32[1,32,8,4,128]{4,1,3,2,0:T(8,128)}, u32[]{:S(2)}) copy-start(f32[1,32,8,4,128]{4,1,3,2,0:T(8,128)} %copy-done.33) | copy-start | bytes 1572868
  99.3 3.0 %copy-start.36 = (f32[1,32,8,4,128]{4,1,3,2,0:T(8,128)S(1)}, f32[1,32,8,4,128]{4,1,3,2,0:T(8,128)}, u32[]{:S(2)}) copy-start(f32[1,32,8,4,128]{4,1,3,2,0:T(8,128)} %copy-done.35) | copy-start | bytes 1572868
  99.3 3.0 %copy-start.46 = (f32[1,32,8,4,128]{4,1,3,2,0:T(8,128)S(1)}, f32[1,32,8,4,128]{4,1,3,2,0:T(8,128)}, u32[]{:S(2)}) copy-start(f32[1,32,8,4,128]{4,1,3,2,0:T(8,128)} %copy-done.45) | copy-start | bytes 1572868
  (42 other events, 66.3 us)
where the time goes:
time: 135 us
  Pallas kernels  45.5 us (34%)
  local copies, waits for them, and re-layouts  41.2 us (31%)
  matrix products  29.9 us (22%)
  other arithmetic  12 us (9%)
  between operations  6.18 us (5%)
    pallas_call x1, Pallas kernels, total_over_tiles(): pl.pallas_call(functools.partial(total_kernel, sizes), out_shape=jax.Shap...  19.4 us
    pallas_call x1, Pallas kernels, opening(): pl.pallas_call(functools.partial(opening_kernel, sizes), out_shape=(jax.S...  18.3 us
    dot_general x18, matrix products, kernel_terms(): jnp.einsum('aizyx,ozyx->aio', stacked, seed, precision=precise)  15.6 us
    dot_general x18, matrix products, convolve(): jnp.einsum('aizyx,aio->ozyx', stacked, kernel[shift_z, shift_y], precisio...  12.3 us
    unnamed x167, local copies, waits for them, and re-layouts  11.8 us
    pallas_call x1, Pallas kernels, line_gather(): pl.pallas_call(functools.partial(line_kernel, sizes), out_shape=jax.Shape...  7.71 us
    select_n x14, local copies, waits for them, and re-layouts, kept(): return value if a == 0 and b == 0 else jnp.where(inside(a, b), value, 0.0)  5.99 us
    another operation x6, local copies, waits for them, and re-layouts, shifted_stack(): jnp.stack([padded[:, shift_z:shift_z + extent_z, shift_y:shift_y + extent...  5.97 us

commit v1 on v0

--- a/solution.py
+++ b/solution.py
@@ -290,6 +290,118 @@
     return tuple(given)
 
 
+def halves(value):
+    high = value.astype(jnp.bfloat16)
+    return high, (value - high.astype(jnp.float32)).astype(jnp.bfloat16)
+
+
+def fine_kernel(whole, faces, edges, weight, seed, hidden, means, gradient, taps, slopes, sums):
+    cores, depth, height, channels, wide = whole.shape
+    inputs = cores * channels
+    outputs = seed.shape[1]
+    span = height * wide
+    lanes = lax.broadcasted_iota(jnp.int32, (inputs, wide), 1)
+    weight_all = jnp.concatenate(halves(weight[...]), axis=0)
+    half = weight_all.shape[0] // 2
+    for z in (0, depth + 1):
+        slopes[z] = jnp.zeros(slopes.shape[1:], slopes.dtype)
+    pooled = []
+
+    def finish(z):
+        value = sums[z]
+        logistic = jax.nn.sigmoid(value)
+        active = value * logistic
+        hidden[z] = active
+        high, rest = halves(seed[z] * (logistic * (1.0 + value * (1.0 - logistic))))
+        slopes[z + 1, :outputs] = high
+        slopes[z + 1, outputs:] = rest
+        rows = sum(active[:, y * wide : (y + 1) * wide] for y in range(height))
+        if z % RATIO == 0:
+            pooled.append(rows)
+        else:
+            pooled[-1] = pooled[-1] + rows
+
+    for z in range(depth):
+        for y in range(height + 2):
+            if y == 0:
+                row = faces[0, :, z]
+            elif y == height + 1:
+                row = faces[1, :, z]
+            else:
+                row = whole[:, z, y - 1]
+            row = row.reshape(inputs, wide)
+            left = jnp.where(lanes == 0, edges[0, z][:, y : y + 1], pltpu.roll(row, 1, 1))
+            right = jnp.where(
+                lanes == wide - 1, edges[1, z][:, y : y + 1], pltpu.roll(row, wide - 1, 1)
+            )
+            high, rest = halves(jnp.concatenate([left, row, right], axis=0))
+            place = slice(y * wide, (y + 1) * wide)
+            taps[z, : 3 * inputs, place] = high
+            taps[z, 3 * inputs :, place] = rest
+        product = jnp.dot(weight_all, taps[z], preferred_element_type=jnp.float32)
+        for dz in range(3):
+            goal = z - dz + 1
+            if not 0 <= goal < depth:
+                continue
+            term = None
+            for dy in range(3):
+                at = (dz * 3 + dy) * outputs
+                for start in (at, half + at):
+                    piece = product[start : start + outputs, dy * wide : dy * wide + span]
+                    term = piece if term is None else term + piece
+            sums[goal] = term if z == max(goal - 1, 0) else sums[goal] + term
+        if z:
+            finish(z - 1)
+    finish(depth - 1)
+    groups = wide // RATIO
+    pool = (
+        lax.broadcasted_iota(jnp.int32, (wide, groups), 0) // RATIO
+        == lax.broadcasted_iota(jnp.int32, (wide, groups), 1)
+    ).astype(jnp.float32)
+    for index, rows in enumerate(pooled):
+        means[index] = jnp.dot(
+            rows, pool, precision=lax.Precision.HIGHEST, preferred_element_type=jnp.float32
+        ) * (1.0 / RATIO**3)
+    for dy in range(3):
+        total = None
+        for z in range(depth):
+            term = lax.dot_general(
+                slopes[z : z + 3].reshape(6 * outputs, span),
+                taps[z, :, dy * wide : dy * wide + span],
+                (((1,), (1,)), ((), ())),
+                preferred_element_type=jnp.float32,
+            )
+            total = term if total is None else total + term
+        for place in range(3):
+            at = place * 2 * outputs
+            gradient[2 - place, dy] = (
+                total[at : at + outputs] + total[at + outputs : at + 2 * outputs]
+            )
+
+
+def fine_pass(whole, faces, edges, weight_fine, seed):
+    cores, depth, height, channels, wide = whole.shape
+    inputs, outputs = weight_fine.shape[3:]
+    weight = weight_fine.transpose(0, 1, 4, 2, 3).reshape(9 * outputs, 3 * inputs)
+    hidden, means, gradient = pl.pallas_call(
+        fine_kernel,
+        out_shape=(
+            jax.ShapeDtypeStruct(seed.shape, jnp.float32),
+            jax.ShapeDtypeStruct((depth // RATIO, outputs, wide // RATIO), jnp.float32),
+            jax.ShapeDtypeStruct((3, 3, outputs, 6 * inputs), jnp.float32),
+        ),
+        in_specs=[IN_VMEM] * 5,
+        out_specs=[IN_VMEM] * 3,
+        scratch_shapes=[
+            pltpu.VMEM((depth, 6 * inputs, (height + 2) * wide), jnp.bfloat16),
+            pltpu.VMEM((depth + 2, 2 * outputs, height * wide), jnp.bfloat16),
+            pltpu.VMEM(seed.shape, jnp.float32),
+        ],
+        compiler_params=pltpu.CompilerParams(vmem_limit_bytes=48 << 20),
+    )(whole, faces, edges, jnp.concatenate([weight, weight], axis=1), seed)
+    return hidden, means, gradient[..., : 3 * inputs] + gradient[..., 3 * inputs :]
+
+
 def as_rows(*arrays):
     return jnp.concatenate([array.reshape(-1, LANES) for array in arrays])
 
@@ -371,26 +483,15 @@
     def edge_piece(a, b):
         edge = sides[key(a, b), :, 1 if b < 0 else 0].reshape(cores * channels, depth, height)
         edge = edge[:, :, -1:] if a < 0 else edge[:, :, :1] if a > 0 else edge
-        return kept(a, b, edge)[..., None]
+        return kept(a, b, edge)
 
     def edge_column(b):
-        return jnp.concatenate([edge_piece(a, b) for a in (-1, 0, 1)], axis=2)
-
-    def face(a):
-        rows = faces[0 if a < 0 else 1].transpose(0, 2, 1, 3).reshape(cores * channels, depth, wide)
-        return kept(a, 0, rows)[:, :, None]
-
-    fine_all = whole.transpose(0, 3, 1, 2, 4).reshape(cores * channels, depth, height, wide)
-    fine_pad = pad_depth(
-        jnp.concatenate(
-            [
-                edge_column(-1),
-                jnp.concatenate([face(-1), fine_all, face(1)], axis=2),
-                edge_column(1),
-            ],
-            axis=3,
-        )
-    )
+        column = jnp.concatenate([edge_piece(a, b) for a in (-1, 0, 1)], axis=2)
+        return column.transpose(1, 0, 2)
+
+    edge_columns = jnp.stack([edge_column(-1), edge_column(1)])
+    known = jnp.stack([inside(-1, 0), inside(1, 0)])[:, None, None, None, None]
+    faces = jnp.where(known, faces, 0.0)
 
     first = coarse_cotangent.size // LANES
     second = first + group_seed.size // LANES
@@ -423,9 +524,16 @@
 
     coarse_pre = convolve(coarse_pad, weight_coarse)
     coarse_hidden = jax.nn.silu(coarse_pre)
-    fine_pre = convolve(fine_pad, weight_fine)
-    fine_hidden = jax.nn.silu(fine_pre)
-    tile_means = group_view(fine_hidden).mean(axis=(2, 4, 6))
+    hidden_seed = fine_seed + refine(tile_seed)
+    fine_hidden, tile_means, fine_terms = fine_pass(
+        whole,
+        faces,
+        edge_columns,
+        weight_fine,
+        hidden_seed.transpose(1, 0, 2, 3).reshape(depth, channels, height * wide),
+    )
+    fine_hidden = fine_hidden.reshape(depth, channels, height, wide).transpose(1, 0, 2, 3)
+    tile_means = tile_means.transpose(1, 0, 2)[:, :, None]
     middle = line_gather(sizes, as_rows(coarse_hidden, tile_means))
     hiddens = middle[:, :, :first].reshape(rows_total, cores * broad, low, short, narrow)
     means = middle[:, :, first:].reshape(rows_total, cores * channels, low, short, narrow)
@@ -445,12 +553,11 @@
     )
     lower_gradient = jnp.einsum("fzyx,czyx->fc", averaged_wide, coarse_seed_own, precision=precise)
     lift_gradient = jnp.einsum("czyx,fzyx->cf", coarse_wide, lifted_seed, precision=precise)
-    hidden_seed = fine_seed + refine(tile_seed)
     coarse_gradient = kernel_terms(coarse_pad, coarse_total_seed * silu_slope(coarse_pre))
-    fine_gradient = kernel_terms(fine_pad, hidden_seed * silu_slope(fine_pre))
-    fine_gradient, coarse_gradient, lift_gradient, lower_gradient = total_over_tiles(
-        sizes, (fine_gradient, coarse_gradient, lift_gradient, lower_gradient)
-    )
+    fine_terms, coarse_gradient, lift_gradient, lower_gradient = total_over_tiles(
+        sizes, (fine_terms, coarse_gradient, lift_gradient, lower_gradient)
+    )
+    fine_gradient = fine_terms.reshape(3, 3, channels, 3, -1).transpose(0, 1, 3, 4, 2)
     return (
         joined_fine,
         joined_coarse,

time: 135 us -> 90.5 us (0.67)
  matrix products: 29.9 us -> 5.52 us
  local copies, waits for them, and re-layouts: 41.2 us -> 23.7 us
  other arithmetic: 12 us -> 6.55 us
  Pallas kernels: 45.5 us -> 48.9 us
    dot_general x18 -> x9, matrix products: 15.6 us -> 1.87 us  [kernel_terms(): jnp.einsum('aizyx,ozyx->aio', stacked, seed, precision=precise)]
    dot_general x18 -> x9, matrix products: 12.3 us -> 1.71 us  [convolve(): jnp.einsum('aizyx,aio->ozyx', stacked, kernel[shift_z, shift_y], precisio...]
    another operation x6 -> x3, local copies, waits for them, and re-layouts: 5.97 us -> 0.24 us  [shifted_stack(): jnp.stack([padded[:, shift_z:shift_z + extent_z, shift_y:shift_y + extent...]
    select_n x14 -> x10, local copies, waits for them, and re-layouts: 5.99 us -> 1.02 us  [kept(): return value if a == 0 and b == 0 else jnp.where(inside(a, b), value, 0.0)]
    unnamed x167 -> x38, local copies, waits for them, and re-layouts: 11.8 us -> 7.52 us
    pallas_call x0 -> x1, Pallas kernels: none -> 3.43 us  [fine_pass(): pl.pallas_call(fine_kernel, out_shape=(jax.ShapeDtypeStruct(seed.shape, j...]
    another operation x6 -> x3, other arithmetic: 2.1 us -> 0.04 us  [shifted_stack(): jnp.stack([padded[:, shift_z:shift_z + extent_z, shift_y:shift_y + extent...]
    mul x1 -> x0, other arithmetic: 1.91 us -> none  [local(): fine_gradient = kernel_terms(fine_pad, hidden_seed * silu_slope(fine_pre))]
where the time goes in v1:
time: 90.5 us; the launch traced here: 90 us
  Pallas kernels  48.9 us (54%)
  local copies, waits for them, and re-layouts  23.7 us (26%)
  other arithmetic  6.55 us (7%)
  matrix products  5.52 us (6%)
  between operations  5.3 us (6%)
    pallas_call x1, Pallas kernels, total_over_tiles(): pl.pallas_call(functools.partial(total_kernel, sizes), out_shape=jax.Shap...  19.4 us
    pallas_call x1, Pallas kernels, opening(): pl.pallas_call(functools.partial(opening_kernel, sizes), out_shape=(jax.S...  18.3 us
    pallas_call x1, Pallas kernels, line_gather(): pl.pallas_call(functools.partial(line_kernel, sizes), out_shape=jax.Shape...  7.72 us
    unnamed x38, local copies, waits for them, and re-layouts  7.52 us
    pallas_call x1, Pallas kernels, fine_pass(): pl.pallas_call(fine_kernel, out_shape=(jax.ShapeDtypeStruct(seed.shape, j...  3.43 us
    slice x3, local copies, waits for them, and re-layouts, total_over_tiles(): given.append(result[start:start + count].reshape(array.shape))  2.55 us
    dot_general x9, matrix products, kernel_terms(): jnp.einsum('aizyx,ozyx->aio', stacked, seed, precision=precise)  1.87 us

profile of v1, /device:TPU:0, one launch (start us, length us, event | category | flops | bytes accessed | tf_op | source)
XLA Modules:
  0.0 90.0 jit_solution(7268272645978308087)
XLA Ops:
  0.7 1.2 %copy.293 = f32[16,8,4,128]{3,0,2,1:T(8,128)S(1)} copy(f32[16,8,4,128]{3,2,1,0:T(4,128)} %param.10) | data formatting | bytes 524288 | tf_op args[0]
  1.8 1.2 %fusion.96 = (f32[16,8,4,1]{3,2,1,0:T(4,128)S(1)}, f32[16,8,4,1]{3,2,1,0:T(4,128)S(1)}) fusion(f32[16,8,4,128]{3,2,1,0:T(4,128)} %param.10), kind=kLoop, calls=%fused_computation.210 | loop fusion | bytes 8192 | tf_op jit(solution)/shard_map/slice | solution.py:445
  3.1 0.3 copy.270
  3.4 0.3 copy.269
  3.9 0.5 broadcast.149
  4.5 0.7 reduce.8
  6.6 18.3 %shard_map.145 = (f32[2,8,4,16,128]{4,3,2,1,0:T(8,128)S(1)}, f32[2,2,8,16,128]{4,3,2,1,0:T(8,128)S(1)}, f32[6,2,24,128]{3,2,1,0:T(8,128)S(1)}, f32[4,2,40,128]{3,2,1,0:T(8,128)S(1)}) custom-call(f32[8,4,16,128]{3,2,1,0:T(8,128)S(1)} %bitcast.410, f32[24,128]{1,0:T(8,128)S(1)} %pad_maximum_fusion.11.near, f32[40,128]{1,0:T(8,128)S(1)} %pad_maximum_fusion.10.line), custom_call_target="tpu_custom_call" | custom-call | tf_op jit(solution)/shard_map/pallas_call | solution.py:173
  25.1 1.6 %reshape.319 = f32[6,2,2,16,8,4]{5,4,3,2,1,0:T(8,128)S(1)} reshape(f32[6,2,8,128]{3,2,1,0:T(8,128)S(1)} %slice.282) | data formatting | bytes 98304 | tf_op jit(solution)/shard_map/reshape | solution.py:455
  26.7 0.8 fusion.94
  27.5 1.1 %copy.274 = f32[32,8,1]{0,1,2:T(8,128)S(1)} copy(f32[32,8,1]{2,1,0:T(8,128)} %bitcast.425) | data formatting | bytes 2048
  28.6 1.0 %slice.356 = f32[32,8,1]{2,1,0:T(8,128)S(1)} slice(f32[32,8,4]{2,1,0:T(8,128)} %bitcast.424), slice={[0:32], [0:8], [3:4]} | slice | bytes 2048 | tf_op jit(solution)/shard_map/slice | solution.py:485
  31.3 0.6 dynamic_slice.35
  33.9 1.3 %fusion.92 = (f32[]{:T(128)}, f32[]{:T(128)}, s32[4,1]{0,1:T(1,128)S(1)}, f32[4,1]{0,1:T(1,128)S(1)}) fusion(s32[]{:T(128)S(6)} %axis_index.33, s32[]{:T(128)} %bitcast.19, s32[4,2]{0,1:T(2,128)S(1)} %copy-done.7, s32[]{:T(128)S(6)} %select_n.190, s32[4,2]{0,1:T(2,128)S(1)} %copy-done.8), kind=kLoop, calls=%fused_computation.206 | loop fusion | flops 26 | bytes 84 | tf_op jit(solution)/shard_map/reduce_sum | solution.py:432
  35.2 0.6 fusion.102
  38.0 3.4 %shard_map.146 = (f32[8,16,512]{2,1,0:T(8,128)S(1)}, f32[2,16,32]{2,1,0:T(8,128)S(1)}, f32[3,3,16,192]{3,2,1,0:T(8,128)S(1)}) custom-call(f32[2,8,4,16,128]{4,3,2,1,0:T(8,128)S(1)} %get-tuple-element.13.whole, f32[2,2,8,16,128]{4,3,2,1,0:T(8,128)S(1)} %broadcast_select_fusion.faces, f32[2,8,32,6]{3,2,1,0:T(8,128)S(1)} %copy.172.edges, ...), custom_call_target="tpu_custom_call" | custom-call | tf_op jit(solution)/shard_map/pallas_call | solution.py:386
  46.3 0.6 pad_maximum_fusion.12.line
  46.9 7.7 %shard_map.147 = f32[4,2,24,128]{3,2,1,0:T(8,128)} custom-call(f32[24,128]{1,0:T(8,128)} %pad_maximum_fusion.12.line), custom_call_target="tpu_custom_call" | custom-call | tf_op jit(solution)/shard_map/pallas_call | solution.py:215
  54.6 0.9 slice.340
  56.4 0.8 bitcast_add_fusion
  57.3 0.4 fusion.19
  58.6 0.7 copy.215
  59.8 0.3 fusion.17
  62.9 0.3 copy.211
  63.6 0.7 select_maximum_fusion
  64.4 19.4 %shard_map.148 = f32[8,72,128]{2,1,0:T(8,128)} custom-call(f32[8,72,128]{2,1,0:T(8,128)} %bitcast.415), custom_call_target="tpu_custom_call" | custom-call | tf_op jit(solution)/shard_map/pallas_call | solution.py:275
  83.8 0.8 slice.386
  84.8 0.7 copy.216
  85.5 1.0 %slice.387 = f32[432,128]{1,0:T(8,128)S(1)} slice(f32[576,128]{1,0:T(8,128)} %bitcast.418), slice={[108:540], [0:128]} | slice | bytes 442368 | tf_op jit(solution)/shard_map/slice | solution.py:288
  86.7 1.1 %copy.217 = f32[3,3,3,64,32]{3,4,2,1,0:T(8,128)} copy(f32[3,3,3,64,32]{4,3,2,1,0:T(8,128)S(1)} %reshape.351) | data formatting | bytes 442368
  87.8 0.8 fusion.95
  88.6 0.7 copy.218
  89.3 0.7 reshape.353
  (155 shorter events, 14.3 us)
Async XLA Ops:
  0.6 3.8 %copy-start.4 = (f32[32,2,1,32]{3,2,1,0:T(1,128)S(1)}, f32[32,2,1,32]{3,2,1,0:T(1,128)}, u32[]{:S(2)}) copy-start(f32[32,2,1,32]{3,2,1,0:T(1,128)} %param.11) | copy-start | bytes 24580
  0.6 4.7 %copy-start.6 = (f32[32,32]{1,0:T(8,128)S(1)}, f32[32,32]{1,0:T(8,128)}, u32[]{:S(2)}) copy-start(f32[32,32]{1,0:T(8,128)} %param.15) | copy-start | bytes 12292
  0.7 4.7 %copy-start.3 = (f32[64,16]{0,1:T(8,128)S(1)}, f32[64,16]{0,1:T(8,128)}, u32[]{:S(2)}) copy-start(f32[64,16]{0,1:T(8,128)} %param.14) | copy-start | bytes 12292
  0.7 4.9 %copy-start = (f32[16,8,4,128]{3,2,1,0:T(4,128)S(1)}, f32[16,8,4,128]{3,2,1,0:T(4,128)}, u32[]{:S(2)}) copy-start(f32[16,8,4,128]{3,2,1,0:T(4,128)} %param.18) | copy-start | bytes 786436
  3.1 3.2 %copy-start.5 = (f32[32,2,1,32]{3,2,1,0:T(1,128)S(1)}, f32[32,2,1,32]{3,2,1,0:T(1,128)}, u32[]{:S(2)}) copy-start(f32[32,2,1,32]{3,2,1,0:T(1,128)} %param.19) | copy-start | bytes 24580
  27.5 3.1 %copy-start.2 = (f32[3,3,3,32,16]{3,4,2,1,0:T(8,128)S(1)}, f32[3,3,3,32,16]{3,4,2,1,0:T(8,128)}, u32[]{:S(2)}) copy-start(f32[3,3,3,32,16]{3,4,2,1,0:T(8,128)} %param.12) | copy-start | bytes 165892
  29.6 1.7 %copy-start.7 = (s32[4,2]{0,1:T(2,128)S(1)}, s32[4,2]{0,1:T(2,128)}, u32[]{:S(2)}) copy-start(s32[4,2]{0,1:T(2,128)} %param.16) | copy-start | bytes 100
  29.9 4.1 %copy-start.8 = (s32[4,2]{0,1:T(2,128)S(1)}, s32[4,2]{0,1:T(2,128)}, u32[]{:S(2)}) copy-start(s32[4,2]{0,1:T(2,128)} %param.17) | copy-start | bytes 100
  42.0 1.7 %copy-start.1 = (f32[3,3,3,64,32]{3,4,2,1,0:T(8,128)S(1)}, f32[3,3,3,64,32]{3,4,2,1,0:T(8,128)}, u32[]{:S(2)}) copy-start(f32[3,3,3,64,32]{3,4,2,1,0:T(8,128)} %param.13) | copy-start | bytes 663556
  54.6 2.6 %slice-start = ((f32[4,2,24,128]{3,2,1,0:T(8,128)}), f32[4,2,8,128]{3,2,1,0:T(8,128)S(1)}, s32[]{:S(2)}) async-start(f32[4,2,24,128]{3,2,1,0:T(8,128)} %shard_map.147), calls=%async_computation | async-start | bytes 65536 | tf_op jit(solution)/shard_map/slice | solution.py:539

commit v2 on v1

--- a/solution.py
+++ b/solution.py
@@ -104,71 +104,118 @@
     pl.semaphore_wait(barrier, len(offsets))
 
 
-def opening_plan(sizes):
+def spread(sizes, kinds):
     rows, columns, cores = sizes
+    assert cores == 2
     plan = []
-    for core in range(1, cores):
-        plan.append(("whole", (0, 0, core)))
-    for core in range(cores):
-        plan.append(("last", (1, 0, core)))
-        plan.append(("first", (rows - 1, 0, core)))
-    for a, b in near_keys(rows, columns):
-        for core in range(cores):
-            if (a, b, core) != (0, 0, 0):
-                plan.append(("near", (a, b, core)))
-    for a in range(rows):
-        for core in range(cores):
-            if (a, core) != (0, 0):
-                plan.append(("line", (a, 0, core)))
+    if "face" in kinds:
+        plan += [("last", (1, 0, 0)), ("first", (rows - 1, 0, 0))]
+    if "line" in kinds:
+        plan += [
+            ("line", (a, b, 0)) for a in range(rows) for b in range(columns) if (a, b) != (0, 0)
+        ]
+    if "near" in kinds:
+        plan += [("near", (a, b, 0)) for a, b in near_keys(rows, columns) if (a, b) != (0, 0)]
     return plan
 
 
 def both_ways(sizes, plan):
-    found = {offset for _, offset in plan}
+    found = {offset for _, offset in plan} | {(0, 0, 1)}
     found |= {tuple((n - s) % n for n, s in zip(sizes, offset)) for offset in found}
     return sorted(found)
 
 
-def opening_kernel(sizes, fine, near, line, whole_out, face_out, near_out, line_out, send, recv):
+def remote(source, goal, send, recv, target):
+    return pltpu.make_async_remote_copy(
+        src_ref=source,
+        dst_ref=goal,
+        send_sem=send,
+        recv_sem=recv,
+        device_id=target,
+        device_id_type=MESH,
+    )
+
+
+def opening_kernel(
+    sizes, fine, near, line, extra, whole_out, face_out, near_out, line_out, extra_out,
+    send, recv, send_on, recv_on, send_own, recv_own,
+):
     rows, columns, _ = sizes
-    plan = opening_plan(sizes)
+    plan = spread(sizes, ("face", "line", "near"))
     keys = near_keys(rows, columns)
-    row_here, core_here = lax.axis_index("gy"), lax.axis_index("col")
+    row_here, column_here, core_here = (lax.axis_index(axis) for axis in AXES)
     greet(sizes, both_ways(sizes, plan))
     height = fine.shape[1]
-    copies = []
+    other = peer(sizes, (0, 0, 1))
+    not_last, not_first = row_here < rows - 1, row_here > 0
+    always = None
+
+    def guarded(condition, action):
+        if condition is always:
+            action()
+        else:
+            pl.when(condition)(action)
+
+    steps = []
     for index, (kind, offset) in enumerate(plan):
-        if kind == "whole":
-            ends = (fine, whole_out.at[core_here])
-        elif kind == "last":
-            ends = (fine.at[:, height - 1], face_out.at[0, core_here])
+        sends = gets = always
+        if kind == "last":
+            source, goal, landed = fine.at[:, height - 1], face_out.at[0, core_here], None
+            sends, gets = not_last, not_first
         elif kind == "first":
-            ends = (fine.at[:, 0], face_out.at[1, core_here])
+            source, goal, landed = fine.at[:, 0], face_out.at[1, core_here], None
+            sends, gets = not_first, not_last
         elif kind == "near":
             slot = keys.index(((rows - offset[0]) % rows, (columns - offset[1]) % columns))
-            ends = (near, near_out.at[slot, core_here])
+            source, goal, landed = near, near_out.at[slot, core_here], None
         else:
-            ends = (line, line_out.at[row_here, core_here])
-        copy = pltpu.make_async_remote_copy(
-            src_ref=ends[0],
-            dst_ref=ends[1],
-            send_sem=send.at[index],
-            recv_sem=recv.at[index],
-            device_id=peer(sizes, offset),
-            device_id_type=MESH,
-        )
+            source, goal = line, line_out.at[row_here, column_here, core_here]
+            origin = peer(sizes, ((rows - offset[0]) % rows, (columns - offset[1]) % columns, 0))
+            landed = line_out.at[origin["gy"], origin["gx"], core_here]
+        landed = goal if landed is None else landed
+        copy = remote(source, goal, send.at[index], recv.at[index], peer(sizes, offset))
+        onward = remote(landed, landed, send_on.at[index], recv_on.at[index], other)
+        guarded(sends, copy.start)
+        steps.append((copy, onward, sends, gets))
+    own = [
+        (near, near_out.at[keys.index((0, 0)), core_here]),
+        (line, line_out.at[row_here, column_here, core_here]),
+        (extra, extra_out.at[core_here]),
+        (fine, whole_out.at[core_here]),
+    ]
+    own = [
+        remote(source, goal, send_own.at[index], recv_own.at[index], other)
+        for index, (source, goal) in enumerate(own)
+    ]
+    for copy in own:
         copy.start()
-        copies.append(copy)
+    near_out[keys.index((0, 0)), core_here] = near[...]
+    line_out[row_here, column_here, core_here] = line[...]
+    extra_out[core_here] = extra[...]
     whole_out[core_here] = fine[...]
-    near_out[keys.index((0, 0)), core_here] = near[...]
-    line_out[row_here, core_here] = line[...]
-    for copy in copies:
+
+    def clear(side):
+        face_out[side] = jnp.zeros(face_out.shape[1:], face_out.dtype)
+
+    pl.when(row_here == 0)(lambda: clear(0))
+    pl.when(row_here == rows - 1)(lambda: clear(1))
+    for copy, onward, _, gets in steps[2:] + steps[:2]:
+
+        def forward(copy=copy, onward=onward):
+            copy.wait_recv()
+            onward.start()
+
+        guarded(gets, forward)
+    for copy, onward, sends, gets in steps:
+        guarded(sends, copy.wait_send)
+        guarded(gets, onward.wait)
+    for copy in own:
         copy.wait()
 
 
-def opening(sizes, fine, near, line):
+def opening(sizes, fine, near, line, extra):
     rows, columns, cores = sizes
-    number = len(opening_plan(sizes))
+    number = len(spread(sizes, ("face", "line", "near")))
     depth, _, channels, wide = fine.shape
     return pl.pallas_call(
         functools.partial(opening_kernel, sizes),
@@ -176,118 +223,103 @@
             jax.ShapeDtypeStruct((cores, *fine.shape), jnp.float32),
             jax.ShapeDtypeStruct((2, cores, depth, channels, wide), jnp.float32),
             jax.ShapeDtypeStruct((len(near_keys(rows, columns)), cores, *near.shape), jnp.float32),
-            jax.ShapeDtypeStruct((rows, cores, *line.shape), jnp.float32),
+            jax.ShapeDtypeStruct((rows, columns, cores, *line.shape), jnp.float32),
+            jax.ShapeDtypeStruct((cores, *extra.shape), jnp.float32),
         ),
-        in_specs=[IN_VMEM] * 3,
-        out_specs=[IN_VMEM] * 4,
-        scratch_shapes=[pltpu.SemaphoreType.DMA((number,)), pltpu.SemaphoreType.DMA((number,))],
+        in_specs=[IN_VMEM] * 4,
+        out_specs=[IN_VMEM] * 5,
+        scratch_shapes=[pltpu.SemaphoreType.DMA((number,))] * 4
+        + [pltpu.SemaphoreType.DMA((4,))] * 2,
         compiler_params=pltpu.CompilerParams(
             collective_id=0, has_side_effects=True, vmem_limit_bytes=48 << 20
         ),
-    )(fine, near, line)
-
-
-def line_kernel(sizes, line, line_out, send, recv):
-    rows, _, cores = sizes
-    offsets = [(a, 0, c) for a in range(rows) for c in range(cores) if (a, c) != (0, 0)]
-    row_here, core_here = lax.axis_index("gy"), lax.axis_index("col")
-    greet(sizes, offsets)
-    copies = []
+    )(fine, near, line, extra)
+
+
+def closing_kernel(
+    sizes, parts, line, result, line_out, landed,
+    send, recv, send_back, recv_back, send_line, recv_line, send_on, recv_on, send_own, recv_own,
+):
+    rows, columns, _ = sizes
+    plan = spread(sizes, ("line",))
+    offsets = [offset for _, offset in plan]
+    row_here, column_here, core_here = (lax.axis_index(axis) for axis in AXES)
+    here = row_here * columns + column_here
+    greet(sizes, both_ways(sizes, plan))
+    other = peer(sizes, (0, 0, 1))
+    own_line = line_out.at[row_here, column_here, core_here]
+    first, lines = [], []
     for index, offset in enumerate(offsets):
-        copy = pltpu.make_async_remote_copy(
-            src_ref=line,
-            dst_ref=line_out.at[row_here, core_here],
-            send_sem=send.at[index],
-            recv_sem=recv.at[index],
-            device_id=peer(sizes, offset),
-            device_id_type=MESH,
+        target = peer(sizes, offset)
+        place = target["gy"] * columns + target["gx"]
+        first.append(
+            remote(parts.at[place], landed.at[index], send.at[index], recv.at[index], target)
         )
+        first[-1].start()
+    for index, offset in enumerate(offsets):
+        origin = peer(sizes, ((rows - offset[0]) % rows, (columns - offset[1]) % columns, 0))
+        arrived = line_out.at[origin["gy"], origin["gx"], core_here]
+        copy = remote(line, own_line, send_line.at[index], recv_line.at[index], peer(sizes, offset))
+        lines.append((copy, remote(arrived, arrived, send_on.at[index], recv_on.at[index], other)))
         copy.start()
-        copies.append(copy)
-    line_out[row_here, core_here] = line[...]
-    for copy in copies:
-        copy.wait()
-
-
-def line_gather(sizes, line):
-    rows, _, cores = sizes
-    number = rows * cores - 1
-    return pl.pallas_call(
-        functools.partial(line_kernel, sizes),
-        out_shape=jax.ShapeDtypeStruct((rows, cores, *line.shape), jnp.float32),
-        in_specs=[IN_VMEM],
-        out_specs=IN_VMEM,
-        scratch_shapes=[pltpu.SemaphoreType.DMA((number,)), pltpu.SemaphoreType.DMA((number,))],
-        compiler_params=pltpu.CompilerParams(collective_id=1, has_side_effects=True),
-    )(line)
-
-
-def total_kernel(sizes, parts, result, landed, send, recv, send_back, recv_back):
-    rows, columns, _ = sizes
-    offsets = [(a, b, 0) for a in range(rows) for b in range(columns) if (a, b) != (0, 0)]
-
-    def place(offset):
-        target = peer(sizes, offset)
-        return target["gy"] * columns + target["gx"]
-
-    here = lax.axis_index("gy") * columns + lax.axis_index("gx")
-    greet(sizes, offsets)
-    copies = []
-    for index, offset in enumerate(offsets):
-        copy = pltpu.make_async_remote_copy(
-            src_ref=parts.at[place(offset)],
-            dst_ref=landed.at[index],
-            send_sem=send.at[index],
-            recv_sem=recv.at[index],
-            device_id=peer(sizes, offset),
-            device_id_type=MESH,
-        )
-        copy.start()
-        copies.append(copy)
+    own = remote(line, own_line, send_own.at[0], recv_own.at[0], other)
+    own.start()
+    line_out[row_here, column_here, core_here] = line[...]
     total = parts[here]
-    for index, copy in enumerate(copies):
+    for index, copy in enumerate(first):
         copy.wait()
         total = total + landed[index]
     result[here] = total
-    copies = []
+    back = []
     for index, offset in enumerate(offsets):
-        copy = pltpu.make_async_remote_copy(
-            src_ref=result.at[here],
-            dst_ref=result.at[here],
-            send_sem=send_back.at[index],
-            recv_sem=recv_back.at[index],
-            device_id=peer(sizes, offset),
-            device_id_type=MESH,
+        back.append(
+            remote(
+                result.at[here],
+                result.at[here],
+                send_back.at[index],
+                recv_back.at[index],
+                peer(sizes, offset),
+            )
         )
-        copy.start()
-        copies.append(copy)
-    for copy in copies:
+        back[-1].start()
+    for copy, onward in lines:
+        copy.wait_recv()
+        onward.start()
+    for copy, onward in lines:
+        copy.wait_send()
+        onward.wait()
+    own.wait()
+    for copy in back:
         copy.wait()
 
 
-def total_over_tiles(sizes, arrays):
-    rows, columns, _ = sizes
+def closing(sizes, arrays, line):
+    rows, columns, cores = sizes
     peers = rows * columns
     flat = jnp.concatenate([array.reshape(-1, LANES) for array in arrays])
     chunk = -(-flat.shape[0] // (8 * peers)) * 8
     parts = jnp.pad(flat, ((0, peers * chunk - flat.shape[0]), (0, 0))).reshape(peers, chunk, LANES)
     number = peers - 1
-    result = pl.pallas_call(
-        functools.partial(total_kernel, sizes),
-        out_shape=jax.ShapeDtypeStruct(parts.shape, jnp.float32),
-        in_specs=[IN_VMEM],
-        out_specs=IN_VMEM,
+    result, lines = pl.pallas_call(
+        functools.partial(closing_kernel, sizes),
+        out_shape=(
+            jax.ShapeDtypeStruct(parts.shape, jnp.float32),
+            jax.ShapeDtypeStruct((rows, columns, cores, *line.shape), jnp.float32),
+        ),
+        in_specs=[IN_VMEM] * 2,
+        out_specs=[IN_VMEM] * 2,
         scratch_shapes=[pltpu.VMEM((number, chunk, LANES), jnp.float32)]
-        + [pltpu.SemaphoreType.DMA((number,))] * 4,
-        compiler_params=pltpu.CompilerParams(collective_id=2, has_side_effects=True),
-    )(parts)
+        + [pltpu.SemaphoreType.DMA((number,))] * 8
+        + [pltpu.SemaphoreType.DMA((1,))] * 2,
+        compiler_params=pltpu.CompilerParams(collective_id=1, has_side_effects=True),
+    )(parts, line)
     result = result.reshape(peers * chunk, LANES)
     given, start = [], 0
     for array in arrays:
         count = array.size // LANES
         given.append(result[start : start + count].reshape(array.shape))
         start += count
-    return tuple(given)
+    return given, lines
 
 
 def halves(value):
@@ -427,9 +459,10 @@
     )
     target = lax.dynamic_slice_in_dim(column_rows, row_here, 1, 0)[0]
     own_count = lax.dynamic_slice_in_dim(column_counts, row_here, 1, 0)[0]
-    routed_here = (column_rows == row_here).astype(jnp.float32)
-    weights_here = routed_here * column_counts
-    divisor_here = jnp.maximum(jnp.sum(weights_here), 1.0)
+    every_row = jnp.arange(rows_total, dtype=jnp.int32)
+    routed = (block_row[None] == every_row[:, None, None]).astype(jnp.float32)
+    weighted = routed * tile_count.astype(jnp.float32)[None]
+    divisors = jnp.maximum(jnp.sum(weighted, axis=1), 1.0)
     divisor_target = jnp.maximum(
         jnp.sum(jnp.where(column_rows == target, column_counts, 0.0)), 1.0
     )
@@ -444,8 +477,9 @@
     fine_rows = fine_in.transpose(1, 2, 0, 3)
     edges = jnp.stack([fine_in[..., 0], fine_in[..., wide - 1]])
     near = as_rows(context_in, edges)
-    line = as_rows(coarse_seed_own, group_seed, lift_weight, lower_weight)
-    whole, faces, nears, lines = opening(sizes, fine_rows, near, line)
+    line = as_rows(coarse_seed_own, group_seed)
+    extra = as_rows(lift_weight, lower_weight)
+    whole, faces, nears, lines, extras = opening(sizes, fine_rows, near, line, extra)
 
     keys = near_keys(rows_total, columns_total)
     context_rows = context_in.size // LANES
@@ -490,22 +524,28 @@
         return column.transpose(1, 0, 2)
 
     edge_columns = jnp.stack([edge_column(-1), edge_column(1)])
-    known = jnp.stack([inside(-1, 0), inside(1, 0)])[:, None, None, None, None]
-    faces = jnp.where(known, faces, 0.0)
 
     first = coarse_cotangent.size // LANES
-    second = first + group_seed.size // LANES
-    third = second + lift_weight.size // LANES
-    seeds = lines[:, :, :first].reshape(rows_total, cores * broad, low, short, narrow)
-    groups = lines[:, :, first:second].reshape(
-        rows_total, cores * channels, low, short, narrow
-    )
-    weights_all = lax.dynamic_index_in_dim(lines, row_here, 0, False)
-    lift_all = weights_all[:, second:third].reshape(cores, *lift_weight.shape)
-    lower_all = weights_all[:, third:].reshape(cores, *lower_weight.shape)
-
-    lifted_seed_all = jnp.einsum("r,rfzyx->fzyx", routed_here, groups, precision=lax.Precision.HIGHEST)
-    lifted_seed = lax.dynamic_slice_in_dim(lifted_seed_all, core_here * channels, channels, 0)
+    lift_rows = lift_weight.size // LANES
+    line_shape = (rows_total, columns_total)
+    seeds = lines[:, :, :, :first].reshape(*line_shape, cores, broad, low, short, narrow)
+    groups = lines[:, :, :, first:].reshape(*line_shape, cores * channels, low, short, narrow)
+    lift_all = extras[:, :lift_rows].reshape(cores, *lift_weight.shape)
+    lower_all = extras[:, lift_rows:].reshape(cores, *lower_weight.shape)
+
+    def routed_sum(factors, values):
+        factors = factors.reshape(*factors.shape, 1, 1, 1, 1)
+        return jnp.sum(factors * values[None], axis=1)
+
+    def block_at(values, row):
+        return lax.dynamic_index_in_dim(
+            lax.dynamic_index_in_dim(values, row, 0, False), column_here, 0, False
+        )
+
+    lifted_seeds = routed_sum(routed, groups)
+    lifted_seed_all = block_at(lifted_seeds, row_here)
+    lifted_seeds_own = lax.dynamic_slice_in_dim(lifted_seeds, core_here * channels, channels, 2)
+    seeds_own = lax.dynamic_index_in_dim(seeds, core_here, 2, False)
     lift_own = lax.dynamic_slice_in_dim(lift_all, core_here * broad, broad, 1)
     coarse_total_seed = coarse_seed_own + jnp.einsum(
         "kcf,kfzyx->czyx",
@@ -514,11 +554,11 @@
         precision=precise,
     )
     lower_own = lax.dynamic_slice_in_dim(lower_all, core_here * channels, channels, 1)
-    target_seed = lax.dynamic_index_in_dim(seeds, target, 0, False)
+    target_seed = block_at(seeds, target)
     tile_seed = jnp.einsum(
         "kfc,kczyx->fzyx",
         lower_own,
-        target_seed.reshape(cores, broad, low, short, narrow),
+        target_seed,
         precision=precise,
     ) * (own_count / (RATIO * RATIO * RATIO) / divisor_target)
 
@@ -534,29 +574,22 @@
     )
     fine_hidden = fine_hidden.reshape(depth, channels, height, wide).transpose(1, 0, 2, 3)
     tile_means = tile_means.transpose(1, 0, 2)[:, :, None]
-    middle = line_gather(sizes, as_rows(coarse_hidden, tile_means))
-    hiddens = middle[:, :, :first].reshape(rows_total, cores * broad, low, short, narrow)
-    means = middle[:, :, first:].reshape(rows_total, cores * channels, low, short, narrow)
-    coarse_wide = lax.dynamic_index_in_dim(hiddens, row_here, 0, False)
+    coarse_gradient = kernel_terms(coarse_pad, coarse_total_seed * silu_slope(coarse_pre))
+    (fine_terms, coarse_gradient), middle = closing(
+        sizes, (fine_terms, coarse_gradient), as_rows(coarse_hidden, tile_means)
+    )
+    hiddens = middle[:, :, :, :first].reshape(*line_shape, cores * broad, low, short, narrow)
+    means = middle[:, :, :, first:].reshape(*line_shape, cores * channels, low, short, narrow)
     chosen = jnp.einsum(
-        "czyx,cf->fzyx",
-        lax.dynamic_index_in_dim(hiddens, target, 0, False),
-        lift_weight,
-        precision=precise,
+        "czyx,cf->fzyx", block_at(hiddens, target), lift_weight, precision=precise
     )
     joined_fine = fine_hidden + refine(chosen)
-    averaged_wide = (
-        jnp.einsum("r,rfzyx->fzyx", weights_here, means, precision=lax.Precision.HIGHEST) / divisor_here
-    )
+    averaged = routed_sum(weighted, means) / divisors[:, :, None, None, None, None]
     joined_coarse = coarse_hidden + jnp.einsum(
-        "fzyx,fc->czyx", averaged_wide, lower_weight, precision=precise
-    )
-    lower_gradient = jnp.einsum("fzyx,czyx->fc", averaged_wide, coarse_seed_own, precision=precise)
-    lift_gradient = jnp.einsum("czyx,fzyx->cf", coarse_wide, lifted_seed, precision=precise)
-    coarse_gradient = kernel_terms(coarse_pad, coarse_total_seed * silu_slope(coarse_pre))
-    fine_terms, coarse_gradient, lift_gradient, lower_gradient = total_over_tiles(
-        sizes, (fine_terms, coarse_gradient, lift_gradient, lower_gradient)
-    )
+        "fzyx,fc->czyx", block_at(averaged, row_here), lower_weight, precision=precise
+    )
+    lower_gradient = jnp.einsum("kifzyx,kiczyx->fc", averaged, seeds_own, precision=precise)
+    lift_gradient = jnp.einsum("kiczyx,kifzyx->cf", hiddens, lifted_seeds_own, precision=precise)
     fine_gradient = fine_terms.reshape(3, 3, channels, 3, -1).transpose(0, 1, 3, 4, 2)
     return (
         joined_fine,

time: 90.5 us -> 77 us (0.85)
  Pallas kernels: 48.9 us -> 37.6 us
  local copies, waits for them, and re-layouts: 23.7 us -> 20.6 us
  matrix products: 5.52 us -> 7.65 us
    pallas_call x2 -> x1, Pallas kernels: 27.1 us -> 21.4 us  [closing(): pl.pallas_call(functools.partial(closing_kernel, sizes), out_shape=(jax.S...]
    pallas_call x1, Pallas kernels: 18.3 us -> 12.8 us  [opening(): pl.pallas_call(functools.partial(opening_kernel, sizes), out_shape=(jax.S...]
    slice x9 -> x7, local copies, waits for them, and re-layouts: 3.42 us -> 1.81 us  [the longest x1 0.92 us: local(): middle[:, :, :, :first]]
    unnamed x38 -> x42, local copies, waits for them, and re-layouts: 7.52 us -> 6.08 us
    dot_general x7 -> x5, matrix products: 1.71 us -> 3.04 us  [the longest x1 0.94 us: local(): jnp.einsum('kiczyx,kifzyx->cf', hiddens, lifted_seeds_own, precision=prec...]
    reshape x11 -> x7, local copies, waits for them, and re-layouts: 2.11 us -> 1.59 us  [the longest x1 0.44 us: local(): lines[:, :, :, :first]]
where the time goes in v2:
time: 77 us; the launch traced here: 76.7 us
  Pallas kernels  37.6 us (49%)
  local copies, waits for them, and re-layouts  20.6 us (27%)
  matrix products  7.65 us (10%)
  other arithmetic  6.14 us (8%)
  between operations  4.71 us (6%)
    pallas_call x1, Pallas kernels, closing(): pl.pallas_call(functools.partial(closing_kernel, sizes), out_shape=(jax.S...  21.4 us
    pallas_call x1, Pallas kernels, opening(): pl.pallas_call(functools.partial(opening_kernel, sizes), out_shape=(jax.S...  12.8 us
    unnamed x42, local copies, waits for them, and re-layouts  6.08 us
    pallas_call x1, Pallas kernels, fine_pass(): pl.pallas_call(fine_kernel, out_shape=(jax.ShapeDtypeStruct(seed.shape, j...  3.43 us
    dot_general x9, matrix products, convolve(): jnp.einsum('aizyx,aio->ozyx', stacked, kernel[shift_z, shift_y], precisio...  2.45 us
    dot_general x9, matrix products, kernel_terms(): jnp.einsum('aizyx,ozyx->aio', stacked, seed, precision=precise)  1.95 us
    reshape x1, local copies, waits for them, and re-layouts, local(): nears[:, :, context_rows:]  1.6 us

profile of v2, /device:TPU:0, one launch (start us, length us, event | category | flops | bytes accessed | tf_op | source)
XLA Modules:
  0.0 76.7 jit_solution(13635591388482357553)
XLA Ops:
  0.7 1.2 %copy.363 = f32[16,8,4,128]{3,0,2,1:T(8,128)S(1)} copy(f32[16,8,4,128]{3,2,1,0:T(4,128)} %param.10) | data formatting | bytes 524288 | tf_op args[0]
  1.8 1.2 %fusion.96 = (f32[16,8,4,1]{3,2,1,0:T(4,128)S(1)}, f32[16,8,4,1]{3,2,1,0:T(4,128)S(1)}) fusion(f32[16,8,4,128]{3,2,1,0:T(4,128)} %param.10), kind=kLoop, calls=%fused_computation.210 | loop fusion | bytes 8192 | tf_op jit(solution)/shard_map/slice | solution.py:478
  3.1 0.3 copy.331
  3.4 0.3 copy.330
  4.0 0.5 broadcast.224
  4.5 0.7 reduce.9
  6.4 12.8 %shard_map.145 = (f32[2,8,4,16,128]{4,3,2,1,0:T(8,128)S(1)}, f32[2,2,8,16,128]{4,3,2,1,0:T(8,128)S(1)}, f32[6,2,24,128]{3,2,1,0:T(8,128)S(1)}, f32[4,2,2,24,128]{4,3,2,1,0:T(8,128)S(1)}, f32[2,16,128]{2,1,0:T(8,128)S(1)}) custom-call(f32[8,4,16,128]{3,2,1,0:T(8,128)S(1)} %bitcast.382, f32[24,128]{1,0:T(8,128)S(1)} %get-tuple-element.102.near, ...), custom_call_target="tpu_custom_call" | custom-call | tf_op jit(solution)/shard_map/pallas_call | solution.py:220
  19.2 1.6 %reshape.343 = f32[6,2,2,16,8,4]{5,4,3,2,1,0:T(8,128)S(1)} reshape(f32[6,2,8,128]{3,2,1,0:T(8,128)S(1)} %slice.276) | data formatting | bytes 98304 | tf_op jit(solution)/shard_map/reshape | solution.py:489
  22.6 0.4 reshape.346
  23.1 0.6 dynamic_slice.44
  25.7 1.3 %fusion.73 = (f32[]{:T(128)}, f32[4,1]{0,1:T(1,128)S(1)}) fusion(s32[4,2]{0,1:T(2,128)S(1)} %copy-done.10, s32[]{:T(128)S(6)} %select_n.199, s32[]{:T(128)} %bitcast.16, s32[4,2]{0,1:T(2,128)S(1)} %copy-done.11), kind=kLoop, calls=%fused_computation.187 | loop fusion | flops 15 | bytes 60 | tf_op jit(solution)/shard_map/reduce_sum | solution.py:467
  27.0 0.6 fusion.101
  29.8 3.4 %shard_map.146 = (f32[8,16,512]{2,1,0:T(8,128)S(1)}, f32[2,16,32]{2,1,0:T(8,128)S(1)}, f32[3,3,16,192]{3,2,1,0:T(8,128)S(1)}) custom-call(f32[2,8,4,16,128]{4,3,2,1,0:T(8,128)S(1)} %get-tuple-element.16.whole, f32[2,2,8,16,128]{4,3,2,1,0:T(8,128)S(1)} %get-tuple-element.17.faces, f32[2,8,32,6]{3,2,1,0:T(8,128)S(1)} %copy.242.edges, ...), custom_call_target="tpu_custom_call" | custom-call | tf_op jit(solution)/shard_map/pallas_call | solution.py:418
  36.1 0.3 copy-done.2
  37.4 0.3 convolution_bitcast_fusion.13
  39.2 0.3 fusion.61
  41.9 0.3 copy.276
  42.7 0.7 select_maximum_fusion
  43.6 0.6 pad_maximum_fusion.12.line
  44.2 21.4 %shard_map.147 = (f32[8,72,128]{2,1,0:T(8,128)}, f32[4,2,2,24,128]{4,3,2,1,0:T(8,128)}) custom-call(f32[8,72,128]{2,1,0:T(8,128)} %bitcast.387, f32[24,128]{1,0:T(8,128)} %pad_maximum_fusion.12.line), custom_call_target="tpu_custom_call" | custom-call | tf_op jit(solution)/shard_map/pallas_call | solution.py:303
  65.7 0.9 %slice.338 = f32[4,2,2,16,128]{4,3,2,1,0:T(8,128)S(1)} slice(f32[4,2,2,24,128]{4,3,2,1,0:T(8,128)} %get-tuple-element.24), slice={[0:4], [0:2], [0:2], [0:16], [0:128]} | slice | bytes 262144 | tf_op jit(solution)/shard_map/slice | solution.py:581
  66.6 0.4 reshape.366
  67.7 0.8 %bitcast_add_fusion = f32[16,8,4,128]{3,2,1,0:T(4,128)} fusion(f32[8,16,4,128]{3,2,1,0:T(4,128)S(1)} %reshape.349, f32[16,8,128]{2,1,0:T(8,128)S(1)} %copy.281), kind=kLoop, calls=%fused_computation.47 | loop fusion | flops 65536 | bytes 589824 | tf_op jit(solution)/shard_map/add | solution.py:586
  68.5 0.8 %slice.339 = f32[4,2,2,8,128]{4,3,2,1,0:T(8,128)S(1)} slice(f32[4,2,2,24,128]{4,3,2,1,0:T(8,128)} %get-tuple-element.24), slice={[0:4], [0:2], [0:2], [16:24], [0:128]} | slice | bytes 131072 | tf_op jit(solution)/shard_map/slice | solution.py:582
  70.1 0.6 dynamic-slice.19
  70.7 0.8 %fusion.1 = f32[32,2,1,32]{3,0,1,2:T(8,128)S(1)} fusion(f32[4,2,32,2,1,32]{5,2,3,1,0,4:T(8,128)S(1)} %bitcast.397, s32[]{:T(128)S(6)} %select_n.198, s32[]{:T(128)S(6)} %select_n.200, f32[1,1]{1,0:T(1,128)} %dynamic-slice.19, f32[32,32]{1,0:T(8,128)S(1)} %copy-done.9, f32[32,2,32]{2,0,1:T(8,128)S(1)} %get-tuple-element.101), kind=kOutput, calls=%fused_computation.11 | convolution fusion | flops 405504 | bytes 90124 | tf_op jit(solution)/shard_map/fzyx,fc->czyx/dot_general | solution.py:588
  71.5 0.6 copy.292
  72.4 0.7 copy.293
  73.3 1.1 %copy.294 = f32[3,3,3,64,32]{3,4,2,1,0:T(8,128)} copy(f32[3,3,3,64,32]{4,3,2,1,0:T(8,128)S(1)} %reshape.370) | data formatting | bytes 442368
  74.4 0.4 reshape.371
  74.8 0.9 %convolution_bitcast_fusion.23 = f32[64,16]{0,1:T(8,128)} fusion(f32[4,2,64,2,32]{4,3,2,1,0:T(2,128)S(1)} %reshape.371, f32[4,2,32,2,32]{4,2,3,1,0:T(8,128)S(1)} %multiply_reduce_fusion.1, s32[]{:T(128)S(6)} %select_n.196), kind=kOutput, calls=%fused_computation.37 | convolution fusion | flops 3145728 | bytes 659460 | tf_op jit(solution)/shard_map/kiczyx,kifzyx->cf/dot_general | solution.py:592
  75.8 0.9 %convolution_bitcast_fusion.22 = f32[32,32]{1,0:T(8,128)} fusion(f32[4,2,1,32,2,1,32]{6,4,3,2,1,0,5:T(2,128)S(1)} %constant_dynamic-slice_fusion, f32[4,2,32,2,32]{4,2,3,1,0:T(8,128)S(1)} %multiply_reduce_fusion, f32[4,2]{1,0:T(4,128)S(1)} %copy.284), kind=kOutput, calls=%fused_computation.36 | convolution fusion | flops 3162112 | bytes 135200 | tf_op jit(solution)/shard_map/kifzyx,kiczyx->fc/dot_general | solution.py:591
  (164 shorter events, 14.1 us)
Async XLA Ops:
  0.6 3.8 %copy-start.6 = (f32[32,2,1,32]{3,2,1,0:T(1,128)S(1)}, f32[32,2,1,32]{3,2,1,0:T(1,128)}, u32[]{:S(2)}) copy-start(f32[32,2,1,32]{3,2,1,0:T(1,128)} %param.11) | copy-start | bytes 24580
  0.6 4.7 %copy-start = (f32[16,8,4,128]{3,2,1,0:T(4,128)S(1)}, f32[16,8,4,128]{3,2,1,0:T(4,128)}, u32[]{:S(2)}) copy-start(f32[16,8,4,128]{3,2,1,0:T(4,128)} %param.18) | copy-start | bytes 786436
  1.8 4.2 %copy-start.7 = (f32[32,2,1,32]{3,2,1,0:T(1,128)S(1)}, f32[32,2,1,32]{3,2,1,0:T(1,128)}, u32[]{:S(2)}) copy-start(f32[32,2,1,32]{3,2,1,0:T(1,128)} %param.19) | copy-start | bytes 24580
  3.1 3.1 %copy-start.9 = (f32[32,32]{1,0:T(8,128)S(1)}, f32[32,32]{1,0:T(8,128)}, u32[]{:S(2)}) copy-start(f32[32,32]{1,0:T(8,128)} %param.15) | copy-start | bytes 12292
  3.1 3.2 %copy-start.5 = (f32[64,16]{0,1:T(8,128)S(1)}, f32[64,16]{0,1:T(8,128)}, u32[]{:S(2)}) copy-start(f32[64,16]{0,1:T(8,128)} %param.14) | copy-start | bytes 12292
  20.9 1.3 %copy-start.4 = (f32[3,3,3,32,16]{3,4,2,1,0:T(8,128)S(1)}, f32[3,3,3,32,16]{3,4,2,1,0:T(8,128)}, u32[]{:S(2)}) copy-start(f32[3,3,3,32,16]{3,4,2,1,0:T(8,128)} %param.12) | copy-start | bytes 165892
  21.6 1.5 %copy-start.10 = (s32[4,2]{0,1:T(2,128)S(1)}, s32[4,2]{0,1:T(2,128)}, u32[]{:S(2)}) copy-start(s32[4,2]{0,1:T(2,128)} %param.16) | copy-start | bytes 100
  21.7 4.0 %copy-start.11 = (s32[4,2]{0,1:T(2,128)S(1)}, s32[4,2]{0,1:T(2,128)}, u32[]{:S(2)}) copy-start(s32[4,2]{0,1:T(2,128)} %param.17) | copy-start | bytes 100
  22.3 7.1 %copy-start.1 = (f32[16,8,4,128]{3,2,1,0:T(4,128)S(1)}, f32[16,8,4,128]{3,2,1,0:T(4,128)}, u32[]{:S(2)}) copy-start(f32[16,8,4,128]{3,2,1,0:T(4,128)} %param.18) | copy-start | bytes 786436
  35.3 1.0 %copy-start.2 = (f32[3,3,3,64,32]{3,4,2,1,0:T(8,128)S(1)}, f32[3,3,3,64,32]{3,4,2,1,0:T(8,128)}, u32[]{:S(2)}) copy-start(f32[3,3,3,64,32]{3,4,2,1,0:T(8,128)} %param.13) | copy-start | bytes 663556
  36.0 3.6 %copy-start.8 = (f32[32,2,1,32]{3,2,1,0:T(1,128)S(1)}, f32[32,2,1,32]{3,2,1,0:T(1,128)}, u32[]{:S(2)}) copy-start(f32[32,2,1,32]{3,2,1,0:T(1,128)} %param.19) | copy-start | bytes 24580
  67.5 4.7 %copy-start.3 = (f32[8,72,128]{2,1,0:T(8,128)S(1)}, f32[8,72,128]{2,1,0:T(8,128)}, u32[]{:S(2)}) copy-start(f32[8,72,128]{2,1,0:T(8,128)} %get-tuple-element.25) | copy-start | bytes 884740

commit v3 on v2

--- a/solution.py
+++ b/solution.py
@@ -237,8 +237,8 @@
 
 
 def closing_kernel(
-    sizes, parts, line, result, line_out, landed,
-    send, recv, send_back, recv_back, send_line, recv_line, send_on, recv_on, send_own, recv_own,
+    sizes, parts, line, result, line_out, landed_x, outgoing, landed_z,
+    send_x, recv_x, send_z, recv_z, back_z, got_z, back_x, got_x, send_line, recv_line, send_on, recv_on, send_own, recv_own,
 ):
     rows, columns, _ = sizes
     plan = spread(sizes, ("line",))
@@ -248,14 +248,26 @@
     greet(sizes, both_ways(sizes, plan))
     other = peer(sizes, (0, 0, 1))
     own_line = line_out.at[row_here, column_here, core_here]
-    first, lines = [], []
-    for index, offset in enumerate(offsets):
-        target = peer(sizes, offset)
-        place = target["gy"] * columns + target["gx"]
-        first.append(
-            remote(parts.at[place], landed.at[index], send.at[index], recv.at[index], target)
-        )
-        first[-1].start()
+    lines = []
+    across = columns - 1
+    order = list(range(1, rows)) + [0]
+
+    def place(a, column):
+        return lax.rem(row_here + a, rows) * columns + column
+
+    sideways = {}
+    for a in order:
+        for b in range(1, columns):
+            index = a * across + b - 1
+            target = peer(sizes, (0, b, 0))
+            sideways[a, b] = remote(
+                parts.at[place(a, target["gx"])],
+                landed_x.at[index],
+                send_x.at[index],
+                recv_x.at[index],
+                target,
+            )
+            sideways[a, b].start()
     for index, offset in enumerate(offsets):
         origin = peer(sizes, ((rows - offset[0]) % rows, (columns - offset[1]) % columns, 0))
         arrived = line_out.at[origin["gy"], origin["gx"], core_here]
@@ -265,23 +277,49 @@
     own = remote(line, own_line, send_own.at[0], recv_own.at[0], other)
     own.start()
     line_out[row_here, column_here, core_here] = line[...]
-    total = parts[here]
-    for index, copy in enumerate(first):
+    along = []
+    for a in order:
+        total = parts[place(a, column_here)]
+        for b in range(1, columns):
+            sideways[a, b].wait()
+            total = total + landed_x[a * across + b - 1]
+        if a:
+            outgoing[a - 1] = total
+            along.append(
+                remote(
+                    outgoing.at[a - 1],
+                    landed_z.at[a - 1],
+                    send_z.at[a - 1],
+                    recv_z.at[a - 1],
+                    peer(sizes, (a, 0, 0)),
+                )
+            )
+            along[-1].start()
+    for index, copy in enumerate(along):
         copy.wait()
-        total = total + landed[index]
+        total = total + landed_z[index]
     result[here] = total
-    back = []
-    for index, offset in enumerate(offsets):
+    back, wide = [], []
+
+    def pass_sideways(a):
+        for b in range(1, columns):
+            index = a * across + b - 1
+            piece = result.at[place(rows - a, column_here)]
+            wide.append(
+                remote(piece, piece, back_x.at[index], got_x.at[index], peer(sizes, (0, b, 0)))
+            )
+            wide[-1].start()
+
+    for a in range(1, rows):
+        piece = result.at[here]
         back.append(
-            remote(
-                result.at[here],
-                result.at[here],
-                send_back.at[index],
-                recv_back.at[index],
-                peer(sizes, offset),
-            )
+            remote(piece, piece, back_z.at[a - 1], got_z.at[a - 1], peer(sizes, (a, 0, 0)))
         )
         back[-1].start()
+    pass_sideways(0)
+    for a in range(1, rows):
+        back[a - 1].wait_recv()
+        pass_sideways(a)
     for copy, onward in lines:
         copy.wait_recv()
         onward.start()
@@ -290,6 +328,8 @@
         onward.wait()
     own.wait()
     for copy in back:
+        copy.wait_send()
+    for copy in wide:
         copy.wait()
 
 
@@ -308,8 +348,15 @@
         ),
         in_specs=[IN_VMEM] * 2,
         out_specs=[IN_VMEM] * 2,
-        scratch_shapes=[pltpu.VMEM((number, chunk, LANES), jnp.float32)]
-        + [pltpu.SemaphoreType.DMA((number,))] * 8
+        scratch_shapes=[
+            pltpu.VMEM((rows * (columns - 1), chunk, LANES), jnp.float32),
+            pltpu.VMEM((rows - 1, chunk, LANES), jnp.float32),
+            pltpu.VMEM((rows - 1, chunk, LANES), jnp.float32),
+        ]
+        + [pltpu.SemaphoreType.DMA((rows * (columns - 1),))] * 2
+        + [pltpu.SemaphoreType.DMA((rows - 1,))] * 4
+        + [pltpu.SemaphoreType.DMA((rows * (columns - 1),))] * 2
+        + [pltpu.SemaphoreType.DMA((number,))] * 4
         + [pltpu.SemaphoreType.DMA((1,))] * 2,
         compiler_params=pltpu.CompilerParams(collective_id=1, has_side_effects=True),
     )(parts, line)

time: 77 us -> 78.8 us (1.023)
  Pallas kernels: 37.6 us -> 39.4 us
    pallas_call x1, Pallas kernels: 21.4 us -> 23.2 us  [closing(): pl.pallas_call(functools.partial(closing_kernel, sizes), out_shape=(jax.S...]
where the time goes in v3:
time: 78.8 us; the launch traced here: 78.5 us
  Pallas kernels  39.4 us (50%)
  local copies, waits for them, and re-layouts  20.6 us (26%)
  matrix products  7.65 us (10%)
  other arithmetic  6.14 us (8%)
  between operations  4.71 us (6%)
    pallas_call x1, Pallas kernels, closing(): pl.pallas_call(functools.partial(closing_kernel, sizes), out_shape=(jax.S...  23.2 us
    pallas_call x1, Pallas kernels, opening(): pl.pallas_call(functools.partial(opening_kernel, sizes), out_shape=(jax.S...  12.8 us
    unnamed x42, local copies, waits for them, and re-layouts  6.08 us
    pallas_call x1, Pallas kernels, fine_pass(): pl.pallas_call(fine_kernel, out_shape=(jax.ShapeDtypeStruct(seed.shape, j...  3.43 us
    dot_general x9, matrix products, convolve(): jnp.einsum('aizyx,aio->ozyx', stacked, kernel[shift_z, shift_y], precisio...  2.45 us
    dot_general x9, matrix products, kernel_terms(): jnp.einsum('aizyx,ozyx->aio', stacked, seed, precision=precise)  1.95 us
    reshape x1, local copies, waits for them, and re-layouts, local(): nears[:, :, context_rows:]  1.6 us

profile of v3, /device:TPU:0, one launch (start us, length us, event | category | flops | bytes accessed | tf_op | source)
XLA Modules:
  0.0 78.5 jit_solution(15222307921988497972)
XLA Ops:
  0.7 1.2 %copy.363 = f32[16,8,4,128]{3,0,2,1:T(8,128)S(1)} copy(f32[16,8,4,128]{3,2,1,0:T(4,128)} %param.10) | data formatting | bytes 524288 | tf_op args[0]
  1.8 1.2 %fusion.96 = (f32[16,8,4,1]{3,2,1,0:T(4,128)S(1)}, f32[16,8,4,1]{3,2,1,0:T(4,128)S(1)}) fusion(f32[16,8,4,128]{3,2,1,0:T(4,128)} %param.10), kind=kLoop, calls=%fused_computation.210 | loop fusion | bytes 8192 | tf_op jit(solution)/shard_map/slice | solution.py:525
  3.1 0.3 copy.331
  3.4 0.3 copy.330
  4.0 0.5 broadcast.224
  4.5 0.7 reduce.9
  6.4 12.8 %shard_map.145 = (f32[2,8,4,16,128]{4,3,2,1,0:T(8,128)S(1)}, f32[2,2,8,16,128]{4,3,2,1,0:T(8,128)S(1)}, f32[6,2,24,128]{3,2,1,0:T(8,128)S(1)}, f32[4,2,2,24,128]{4,3,2,1,0:T(8,128)S(1)}, f32[2,16,128]{2,1,0:T(8,128)S(1)}) custom-call(f32[8,4,16,128]{3,2,1,0:T(8,128)S(1)} %bitcast.382, f32[24,128]{1,0:T(8,128)S(1)} %get-tuple-element.102.near, ...), custom_call_target="tpu_custom_call" | custom-call | tf_op jit(solution)/shard_map/pallas_call | solution.py:220
  19.2 1.6 %reshape.343 = f32[6,2,2,16,8,4]{5,4,3,2,1,0:T(8,128)S(1)} reshape(f32[6,2,8,128]{3,2,1,0:T(8,128)S(1)} %slice.276) | data formatting | bytes 98304 | tf_op jit(solution)/shard_map/reshape | solution.py:536
  22.6 0.4 reshape.346
  23.1 0.6 dynamic_slice.44
  25.7 1.3 %fusion.73 = (f32[]{:T(128)}, f32[4,1]{0,1:T(1,128)S(1)}) fusion(s32[4,2]{0,1:T(2,128)S(1)} %copy-done.10, s32[]{:T(128)S(6)} %select_n.199, s32[]{:T(128)} %bitcast.16, s32[4,2]{0,1:T(2,128)S(1)} %copy-done.11), kind=kLoop, calls=%fused_computation.187 | loop fusion | flops 15 | bytes 60 | tf_op jit(solution)/shard_map/reduce_sum | solution.py:514
  27.0 0.6 fusion.101
  29.8 3.4 %shard_map.146 = (f32[8,16,512]{2,1,0:T(8,128)S(1)}, f32[2,16,32]{2,1,0:T(8,128)S(1)}, f32[3,3,16,192]{3,2,1,0:T(8,128)S(1)}) custom-call(f32[2,8,4,16,128]{4,3,2,1,0:T(8,128)S(1)} %get-tuple-element.16.whole, f32[2,2,8,16,128]{4,3,2,1,0:T(8,128)S(1)} %get-tuple-element.17.faces, f32[2,8,32,6]{3,2,1,0:T(8,128)S(1)} %copy.242.edges, ...), custom_call_target="tpu_custom_call" | custom-call | tf_op jit(solution)/shard_map/pallas_call | solution.py:465
  36.1 0.3 copy-done.2
  37.4 0.3 convolution_bitcast_fusion.13
  39.2 0.3 fusion.61
  41.9 0.3 copy.276
  42.7 0.7 select_maximum_fusion
  43.6 0.6 pad_maximum_fusion.12.line
  44.2 23.2 %shard_map.147 = (f32[8,72,128]{2,1,0:T(8,128)}, f32[4,2,2,24,128]{4,3,2,1,0:T(8,128)}) custom-call(f32[8,72,128]{2,1,0:T(8,128)} %bitcast.387, f32[24,128]{1,0:T(8,128)} %pad_maximum_fusion.12.line), custom_call_target="tpu_custom_call" | custom-call | tf_op jit(solution)/shard_map/pallas_call | solution.py:343
  67.4 0.9 %slice.338 = f32[4,2,2,16,128]{4,3,2,1,0:T(8,128)S(1)} slice(f32[4,2,2,24,128]{4,3,2,1,0:T(8,128)} %get-tuple-element.24), slice={[0:4], [0:2], [0:2], [0:16], [0:128]} | slice | bytes 262144 | tf_op jit(solution)/shard_map/slice | solution.py:628
  68.4 0.4 reshape.366
  69.5 0.8 %bitcast_add_fusion = f32[16,8,4,128]{3,2,1,0:T(4,128)} fusion(f32[8,16,4,128]{3,2,1,0:T(4,128)S(1)} %reshape.349, f32[16,8,128]{2,1,0:T(8,128)S(1)} %copy.281), kind=kLoop, calls=%fused_computation.47 | loop fusion | flops 65536 | bytes 589824 | tf_op jit(solution)/shard_map/add | solution.py:633
  70.2 0.8 %slice.339 = f32[4,2,2,8,128]{4,3,2,1,0:T(8,128)S(1)} slice(f32[4,2,2,24,128]{4,3,2,1,0:T(8,128)} %get-tuple-element.24), slice={[0:4], [0:2], [0:2], [16:24], [0:128]} | slice | bytes 131072 | tf_op jit(solution)/shard_map/slice | solution.py:629
  71.9 0.6 dynamic-slice.19
  72.5 0.8 %fusion.1 = f32[32,2,1,32]{3,0,1,2:T(8,128)S(1)} fusion(f32[4,2,32,2,1,32]{5,2,3,1,0,4:T(8,128)S(1)} %bitcast.397, s32[]{:T(128)S(6)} %select_n.198, s32[]{:T(128)S(6)} %select_n.200, f32[1,1]{1,0:T(1,128)} %dynamic-slice.19, f32[32,32]{1,0:T(8,128)S(1)} %copy-done.9, f32[32,2,32]{2,0,1:T(8,128)S(1)} %get-tuple-element.101), kind=kOutput, calls=%fused_computation.11 | convolution fusion | flops 405504 | bytes 90124 | tf_op jit(solution)/shard_map/fzyx,fc->czyx/dot_general | solution.py:635
  73.3 0.6 copy.292
  74.2 0.7 copy.293
  75.1 1.1 %copy.294 = f32[3,3,3,64,32]{3,4,2,1,0:T(8,128)} copy(f32[3,3,3,64,32]{4,3,2,1,0:T(8,128)S(1)} %reshape.370) | data formatting | bytes 442368
  76.2 0.4 reshape.371
  76.6 0.9 %convolution_bitcast_fusion.23 = f32[64,16]{0,1:T(8,128)} fusion(f32[4,2,64,2,32]{4,3,2,1,0:T(2,128)S(1)} %reshape.371, f32[4,2,32,2,32]{4,2,3,1,0:T(8,128)S(1)} %multiply_reduce_fusion.1, s32[]{:T(128)S(6)} %select_n.196), kind=kOutput, calls=%fused_computation.37 | convolution fusion | flops 3145728 | bytes 659460 | tf_op jit(solution)/shard_map/kiczyx,kifzyx->cf/dot_general | solution.py:639
  77.6 0.9 %convolution_bitcast_fusion.22 = f32[32,32]{1,0:T(8,128)} fusion(f32[4,2,1,32,2,1,32]{6,4,3,2,1,0,5:T(2,128)S(1)} %constant_dynamic-slice_fusion, f32[4,2,32,2,32]{4,2,3,1,0:T(8,128)S(1)} %multiply_reduce_fusion, f32[4,2]{1,0:T(4,128)S(1)} %copy.284), kind=kOutput, calls=%fused_computation.36 | convolution fusion | flops 3162112 | bytes 135200 | tf_op jit(solution)/shard_map/kifzyx,kiczyx->fc/dot_general | solution.py:638
  (164 shorter events, 14.1 us)
Async XLA Ops:
  0.6 3.8 %copy-start.6 = (f32[32,2,1,32]{3,2,1,0:T(1,128)S(1)}, f32[32,2,1,32]{3,2,1,0:T(1,128)}, u32[]{:S(2)}) copy-start(f32[32,2,1,32]{3,2,1,0:T(1,128)} %param.11) | copy-start | bytes 24580
  0.6 4.7 %copy-start = (f32[16,8,4,128]{3,2,1,0:T(4,128)S(1)}, f32[16,8,4,128]{3,2,1,0:T(4,128)}, u32[]{:S(2)}) copy-start(f32[16,8,4,128]{3,2,1,0:T(4,128)} %param.18) | copy-start | bytes 786436
  1.8 4.2 %copy-start.7 = (f32[32,2,1,32]{3,2,1,0:T(1,128)S(1)}, f32[32,2,1,32]{3,2,1,0:T(1,128)}, u32[]{:S(2)}) copy-start(f32[32,2,1,32]{3,2,1,0:T(1,128)} %param.19) | copy-start | bytes 24580
  3.1 3.1 %copy-start.9 = (f32[32,32]{1,0:T(8,128)S(1)}, f32[32,32]{1,0:T(8,128)}, u32[]{:S(2)}) copy-start(f32[32,32]{1,0:T(8,128)} %param.15) | copy-start | bytes 12292
  3.1 3.2 %copy-start.5 = (f32[64,16]{0,1:T(8,128)S(1)}, f32[64,16]{0,1:T(8,128)}, u32[]{:S(2)}) copy-start(f32[64,16]{0,1:T(8,128)} %param.14) | copy-start | bytes 12292
  20.9 1.3 %copy-start.4 = (f32[3,3,3,32,16]{3,4,2,1,0:T(8,128)S(1)}, f32[3,3,3,32,16]{3,4,2,1,0:T(8,128)}, u32[]{:S(2)}) copy-start(f32[3,3,3,32,16]{3,4,2,1,0:T(8,128)} %param.12) | copy-start | bytes 165892
  21.6 1.5 %copy-start.10 = (s32[4,2]{0,1:T(2,128)S(1)}, s32[4,2]{0,1:T(2,128)}, u32[]{:S(2)}) copy-start(s32[4,2]{0,1:T(2,128)} %param.16) | copy-start | bytes 100
  21.7 4.0 %copy-start.11 = (s32[4,2]{0,1:T(2,128)S(1)}, s32[4,2]{0,1:T(2,128)}, u32[]{:S(2)}) copy-start(s32[4,2]{0,1:T(2,128)} %param.17) | copy-start | bytes 100
  22.3 7.1 %copy-start.1 = (f32[16,8,4,128]{3,2,1,0:T(4,128)S(1)}, f32[16,8,4,128]{3,2,1,0:T(4,128)}, u32[]{:S(2)}) copy-start(f32[16,8,4,128]{3,2,1,0:T(4,128)} %param.18) | copy-start | bytes 786436
  35.3 1.0 %copy-start.2 = (f32[3,3,3,64,32]{3,4,2,1,0:T(8,128)S(1)}, f32[3,3,3,64,32]{3,4,2,1,0:T(8,128)}, u32[]{:S(2)}) copy-start(f32[3,3,3,64,32]{3,4,2,1,0:T(8,128)} %param.13) | copy-start | bytes 663556
  36.0 3.6 %copy-start.8 = (f32[32,2,1,32]{3,2,1,0:T(1,128)S(1)}, f32[32,2,1,32]{3,2,1,0:T(1,128)}, u32[]{:S(2)}) copy-start(f32[32,2,1,32]{3,2,1,0:T(1,128)} %param.19) | copy-start | bytes 24580
  69.3 4.7 %copy-start.3 = (f32[8,72,128]{2,1,0:T(8,128)S(1)}, f32[8,72,128]{2,1,0:T(8,128)}, u32[]{:S(2)}) copy-start(f32[8,72,128]{2,1,0:T(8,128)} %get-tuple-element.25) | copy-start | bytes 884740

commit v4 on v2

--- a/solution.py
+++ b/solution.py
@@ -250,21 +250,24 @@
     own_line = line_out.at[row_here, column_here, core_here]
     first, lines = [], []
     for index, offset in enumerate(offsets):
+        origin = peer(sizes, ((rows - offset[0]) % rows, (columns - offset[1]) % columns, 0))
+        arrived = line_out.at[origin["gy"], origin["gx"], core_here]
+        copy = remote(line, own_line, send_line.at[index], recv_line.at[index], peer(sizes, offset))
+        lines.append((copy, remote(arrived, arrived, send_on.at[index], recv_on.at[index], other)))
+        copy.start()
+    for index, offset in enumerate(offsets):
         target = peer(sizes, offset)
         place = target["gy"] * columns + target["gx"]
         first.append(
             remote(parts.at[place], landed.at[index], send.at[index], recv.at[index], target)
         )
         first[-1].start()
-    for index, offset in enumerate(offsets):
-        origin = peer(sizes, ((rows - offset[0]) % rows, (columns - offset[1]) % columns, 0))
-        arrived = line_out.at[origin["gy"], origin["gx"], core_here]
-        copy = remote(line, own_line, send_line.at[index], recv_line.at[index], peer(sizes, offset))
-        lines.append((copy, remote(arrived, arrived, send_on.at[index], recv_on.at[index], other)))
-        copy.start()
     own = remote(line, own_line, send_own.at[0], recv_own.at[0], other)
     own.start()
     line_out[row_here, column_here, core_here] = line[...]
+    for copy, onward in lines:
+        copy.wait_recv()
+        onward.start()
     total = parts[here]
     for index, copy in enumerate(first):
         copy.wait()
@@ -282,9 +285,6 @@
             )
         )
         back[-1].start()
-    for copy, onward in lines:
-        copy.wait_recv()
-        onward.start()
     for copy, onward in lines:
         copy.wait_send()
         onward.wait()

time: 77 us -> 78.4 us (1.018)
  Pallas kernels: 37.6 us -> 38.9 us
    pallas_call x1, Pallas kernels: 21.4 us -> 22.7 us  [closing(): pl.pallas_call(functools.partial(closing_kernel, sizes), out_shape=(jax.S...]
where the time goes in v4:
time: 78.4 us; the launch traced here: 78 us
  Pallas kernels  38.9 us (50%)
  local copies, waits for them, and re-layouts  20.6 us (26%)
  matrix products  7.65 us (10%)
  other arithmetic  6.14 us (8%)
  between operations  4.71 us (6%)
    pallas_call x1, Pallas kernels, closing(): pl.pallas_call(functools.partial(closing_kernel, sizes), out_shape=(jax.S...  22.7 us
    pallas_call x1, Pallas kernels, opening(): pl.pallas_call(functools.partial(opening_kernel, sizes), out_shape=(jax.S...  12.8 us
    unnamed x42, local copies, waits for them, and re-layouts  6.08 us
    pallas_call x1, Pallas kernels, fine_pass(): pl.pallas_call(fine_kernel, out_shape=(jax.ShapeDtypeStruct(seed.shape, j...  3.43 us
    dot_general x9, matrix products, convolve(): jnp.einsum('aizyx,aio->ozyx', stacked, kernel[shift_z, shift_y], precisio...  2.45 us
    dot_general x9, matrix products, kernel_terms(): jnp.einsum('aizyx,ozyx->aio', stacked, seed, precision=precise)  1.95 us
    reshape x1, local copies, waits for them, and re-layouts, local(): nears[:, :, context_rows:]  1.6 us

profile of v4, /device:TPU:0, one launch (start us, length us, event | category | flops | bytes accessed | tf_op | source)
XLA Modules:
  0.0 78.0 jit_solution(599666979679837313)
XLA Ops:
  0.7 1.2 %copy.363 = f32[16,8,4,128]{3,0,2,1:T(8,128)S(1)} copy(f32[16,8,4,128]{3,2,1,0:T(4,128)} %param.10) | data formatting | bytes 524288 | tf_op args[0]
  1.8 1.2 %fusion.96 = (f32[16,8,4,1]{3,2,1,0:T(4,128)S(1)}, f32[16,8,4,1]{3,2,1,0:T(4,128)S(1)}) fusion(f32[16,8,4,128]{3,2,1,0:T(4,128)} %param.10), kind=kLoop, calls=%fused_computation.210 | loop fusion | bytes 8192 | tf_op jit(solution)/shard_map/slice | solution.py:478
  3.1 0.3 copy.331
  3.4 0.3 copy.330
  4.0 0.5 broadcast.224
  4.5 0.7 reduce.9
  6.4 12.8 %shard_map.145 = (f32[2,8,4,16,128]{4,3,2,1,0:T(8,128)S(1)}, f32[2,2,8,16,128]{4,3,2,1,0:T(8,128)S(1)}, f32[6,2,24,128]{3,2,1,0:T(8,128)S(1)}, f32[4,2,2,24,128]{4,3,2,1,0:T(8,128)S(1)}, f32[2,16,128]{2,1,0:T(8,128)S(1)}) custom-call(f32[8,4,16,128]{3,2,1,0:T(8,128)S(1)} %bitcast.382, f32[24,128]{1,0:T(8,128)S(1)} %get-tuple-element.102.near, ...), custom_call_target="tpu_custom_call" | custom-call | tf_op jit(solution)/shard_map/pallas_call | solution.py:220
  19.2 1.6 %reshape.343 = f32[6,2,2,16,8,4]{5,4,3,2,1,0:T(8,128)S(1)} reshape(f32[6,2,8,128]{3,2,1,0:T(8,128)S(1)} %slice.276) | data formatting | bytes 98304 | tf_op jit(solution)/shard_map/reshape | solution.py:489
  22.6 0.4 reshape.346
  23.1 0.6 dynamic_slice.44
  25.7 1.3 %fusion.73 = (f32[]{:T(128)}, f32[4,1]{0,1:T(1,128)S(1)}) fusion(s32[4,2]{0,1:T(2,128)S(1)} %copy-done.10, s32[]{:T(128)S(6)} %select_n.199, s32[]{:T(128)} %bitcast.16, s32[4,2]{0,1:T(2,128)S(1)} %copy-done.11), kind=kLoop, calls=%fused_computation.187 | loop fusion | flops 15 | bytes 60 | tf_op jit(solution)/shard_map/reduce_sum | solution.py:467
  27.0 0.6 fusion.101
  29.8 3.4 %shard_map.146 = (f32[8,16,512]{2,1,0:T(8,128)S(1)}, f32[2,16,32]{2,1,0:T(8,128)S(1)}, f32[3,3,16,192]{3,2,1,0:T(8,128)S(1)}) custom-call(f32[2,8,4,16,128]{4,3,2,1,0:T(8,128)S(1)} %get-tuple-element.16.whole, f32[2,2,8,16,128]{4,3,2,1,0:T(8,128)S(1)} %get-tuple-element.17.faces, f32[2,8,32,6]{3,2,1,0:T(8,128)S(1)} %copy.242.edges, ...), custom_call_target="tpu_custom_call" | custom-call | tf_op jit(solution)/shard_map/pallas_call | solution.py:418
  36.1 0.3 copy-done.2
  37.4 0.3 convolution_bitcast_fusion.13
  39.2 0.3 fusion.61
  41.9 0.3 copy.276
  42.7 0.7 select_maximum_fusion
  43.6 0.6 pad_maximum_fusion.12.line
  44.2 22.7 %shard_map.147 = (f32[8,72,128]{2,1,0:T(8,128)}, f32[4,2,2,24,128]{4,3,2,1,0:T(8,128)}) custom-call(f32[8,72,128]{2,1,0:T(8,128)} %bitcast.387, f32[24,128]{1,0:T(8,128)} %pad_maximum_fusion.12.line), custom_call_target="tpu_custom_call" | custom-call | tf_op jit(solution)/shard_map/pallas_call | solution.py:303
  67.0 0.9 %slice.338 = f32[4,2,2,16,128]{4,3,2,1,0:T(8,128)S(1)} slice(f32[4,2,2,24,128]{4,3,2,1,0:T(8,128)} %get-tuple-element.24), slice={[0:4], [0:2], [0:2], [0:16], [0:128]} | slice | bytes 262144 | tf_op jit(solution)/shard_map/slice | solution.py:581
  67.9 0.4 reshape.366
  69.0 0.8 %bitcast_add_fusion = f32[16,8,4,128]{3,2,1,0:T(4,128)} fusion(f32[8,16,4,128]{3,2,1,0:T(4,128)S(1)} %reshape.349, f32[16,8,128]{2,1,0:T(8,128)S(1)} %copy.281), kind=kLoop, calls=%fused_computation.47 | loop fusion | flops 65536 | bytes 589824 | tf_op jit(solution)/shard_map/add | solution.py:586
  69.8 0.8 %slice.339 = f32[4,2,2,8,128]{4,3,2,1,0:T(8,128)S(1)} slice(f32[4,2,2,24,128]{4,3,2,1,0:T(8,128)} %get-tuple-element.24), slice={[0:4], [0:2], [0:2], [16:24], [0:128]} | slice | bytes 131072 | tf_op jit(solution)/shard_map/slice | solution.py:582
  71.4 0.6 dynamic-slice.19
  72.0 0.8 %fusion.1 = f32[32,2,1,32]{3,0,1,2:T(8,128)S(1)} fusion(f32[4,2,32,2,1,32]{5,2,3,1,0,4:T(8,128)S(1)} %bitcast.397, s32[]{:T(128)S(6)} %select_n.198, s32[]{:T(128)S(6)} %select_n.200, f32[1,1]{1,0:T(1,128)} %dynamic-slice.19, f32[32,32]{1,0:T(8,128)S(1)} %copy-done.9, f32[32,2,32]{2,0,1:T(8,128)S(1)} %get-tuple-element.101), kind=kOutput, calls=%fused_computation.11 | convolution fusion | flops 405504 | bytes 90124 | tf_op jit(solution)/shard_map/fzyx,fc->czyx/dot_general | solution.py:588
  72.8 0.6 copy.292
  73.7 0.7 copy.293
  74.6 1.1 %copy.294 = f32[3,3,3,64,32]{3,4,2,1,0:T(8,128)} copy(f32[3,3,3,64,32]{4,3,2,1,0:T(8,128)S(1)} %reshape.370) | data formatting | bytes 442368
  75.7 0.4 reshape.371
  76.1 0.9 %convolution_bitcast_fusion.23 = f32[64,16]{0,1:T(8,128)} fusion(f32[4,2,64,2,32]{4,3,2,1,0:T(2,128)S(1)} %reshape.371, f32[4,2,32,2,32]{4,2,3,1,0:T(8,128)S(1)} %multiply_reduce_fusion.1, s32[]{:T(128)S(6)} %select_n.196), kind=kOutput, calls=%fused_computation.37 | convolution fusion | flops 3145728 | bytes 659460 | tf_op jit(solution)/shard_map/kiczyx,kifzyx->cf/dot_general | solution.py:592
  77.1 0.9 %convolution_bitcast_fusion.22 = f32[32,32]{1,0:T(8,128)} fusion(f32[4,2,1,32,2,1,32]{6,4,3,2,1,0,5:T(2,128)S(1)} %constant_dynamic-slice_fusion, f32[4,2,32,2,32]{4,2,3,1,0:T(8,128)S(1)} %multiply_reduce_fusion, f32[4,2]{1,0:T(4,128)S(1)} %copy.284), kind=kOutput, calls=%fused_computation.36 | convolution fusion | flops 3162112 | bytes 135200 | tf_op jit(solution)/shard_map/kifzyx,kiczyx->fc/dot_general | solution.py:591
  (164 shorter events, 14.1 us)
Async XLA Ops:
  0.6 3.8 %copy-start.6 = (f32[32,2,1,32]{3,2,1,0:T(1,128)S(1)}, f32[32,2,1,32]{3,2,1,0:T(1,128)}, u32[]{:S(2)}) copy-start(f32[32,2,1,32]{3,2,1,0:T(1,128)} %param.11) | copy-start | bytes 24580
  0.6 4.7 %copy-start = (f32[16,8,4,128]{3,2,1,0:T(4,128)S(1)}, f32[16,8,4,128]{3,2,1,0:T(4,128)}, u32[]{:S(2)}) copy-start(f32[16,8,4,128]{3,2,1,0:T(4,128)} %param.18) | copy-start | bytes 786436
  1.8 4.2 %copy-start.7 = (f32[32,2,1,32]{3,2,1,0:T(1,128)S(1)}, f32[32,2,1,32]{3,2,1,0:T(1,128)}, u32[]{:S(2)}) copy-start(f32[32,2,1,32]{3,2,1,0:T(1,128)} %param.19) | copy-start | bytes 24580
  3.1 3.1 %copy-start.9 = (f32[32,32]{1,0:T(8,128)S(1)}, f32[32,32]{1,0:T(8,128)}, u32[]{:S(2)}) copy-start(f32[32,32]{1,0:T(8,128)} %param.15) | copy-start | bytes 12292
  3.1 3.2 %copy-start.5 = (f32[64,16]{0,1:T(8,128)S(1)}, f32[64,16]{0,1:T(8,128)}, u32[]{:S(2)}) copy-start(f32[64,16]{0,1:T(8,128)} %param.14) | copy-start | bytes 12292
  20.9 1.3 %copy-start.4 = (f32[3,3,3,32,16]{3,4,2,1,0:T(8,128)S(1)}, f32[3,3,3,32,16]{3,4,2,1,0:T(8,128)}, u32[]{:S(2)}) copy-start(f32[3,3,3,32,16]{3,4,2,1,0:T(8,128)} %param.12) | copy-start | bytes 165892
  21.6 1.5 %copy-start.10 = (s32[4,2]{0,1:T(2,128)S(1)}, s32[4,2]{0,1:T(2,128)}, u32[]{:S(2)}) copy-start(s32[4,2]{0,1:T(2,128)} %param.16) | copy-start | bytes 100
  21.7 4.0 %copy-start.11 = (s32[4,2]{0,1:T(2,128)S(1)}, s32[4,2]{0,1:T(2,128)}, u32[]{:S(2)}) copy-start(s32[4,2]{0,1:T(2,128)} %param.17) | copy-start | bytes 100
  22.3 7.1 %copy-start.1 = (f32[16,8,4,128]{3,2,1,0:T(4,128)S(1)}, f32[16,8,4,128]{3,2,1,0:T(4,128)}, u32[]{:S(2)}) copy-start(f32[16,8,4,128]{3,2,1,0:T(4,128)} %param.18) | copy-start | bytes 786436
  35.3 1.0 %copy-start.2 = (f32[3,3,3,64,32]{3,4,2,1,0:T(8,128)S(1)}, f32[3,3,3,64,32]{3,4,2,1,0:T(8,128)}, u32[]{:S(2)}) copy-start(f32[3,3,3,64,32]{3,4,2,1,0:T(8,128)} %param.13) | copy-start | bytes 663556
  36.0 3.6 %copy-start.8 = (f32[32,2,1,32]{3,2,1,0:T(1,128)S(1)}, f32[32,2,1,32]{3,2,1,0:T(1,128)}, u32[]{:S(2)}) copy-start(f32[32,2,1,32]{3,2,1,0:T(1,128)} %param.19) | copy-start | bytes 24580
  68.8 4.7 %copy-start.3 = (f32[8,72,128]{2,1,0:T(8,128)S(1)}, f32[8,72,128]{2,1,0:T(8,128)}, u32[]{:S(2)}) copy-start(f32[8,72,128]{2,1,0:T(8,128)} %get-tuple-element.25) | copy-start | bytes 884740
